TPU v7x, 128 devices: a whole 4x4x4 slice. The times are simulated.
128 devices in a mesh: clip: 64 (over y, x, z_hi, core), seq: 2 (over z_lo).
Axes of the slice: x: 4, y: 4, z: 4 (z_hi: 2, z_lo: 2; z = z_hi * 2 + z_lo), core: 2. Of those that a mesh axis runs over, the one named last changes fastest.
Arguments:
- latent_tokens: bfloat16 [64, 256, 1536], P('clip', 'seq'), may hold values from -6 to 6
- time_embed: float32 [64, 6, 1536], P('clip'), may hold values from -4 to 4
- text_tokens: bfloat16 [64, 512, 1536], P('clip', 'seq'), may hold values from -6 to 6
- positions: int32 [64, 3, 256], P('clip', None, 'seq'), may hold values from 0 to 30, as said below
- w_qkv: bfloat16 [1536, 4608], P(('clip', 'seq')), may hold values from -0.15625 to 0.15625
- attn_out: bfloat16 [1536, 1536], P(('clip', 'seq')), may hold values from -1.5 to 1.5
- cross_q: bfloat16 [1536, 1536], P(('clip', 'seq')), may hold values from -0.15625 to 0.15625
- cross_kv: bfloat16 [1536, 3072], P(('clip', 'seq')), may hold values from -0.15625 to 0.15625
- cross_out: bfloat16 [1536, 1536], P(('clip', 'seq')), may hold values from -2 to 2
- mlp_in: bfloat16 [1536, 8960], P(('clip', 'seq')), may hold values from -0.15625 to 0.15625
- mlp_out: bfloat16 [8960, 1536], P(('clip', 'seq')), may hold values from -0.0625 to 0.0625
- gain_q: bfloat16 [1536], P(('clip', 'seq')), may hold values from 0.5 to 1.5
- gain_k: bfloat16 [1536], P(('clip', 'seq')), may hold values from 0.5 to 1.5
- gain_cq: bfloat16 [1536], P(('clip', 'seq')), may hold values from 0.5 to 1.5
- gain_ck: bfloat16 [1536], P(('clip', 'seq')), may hold values from 0.5 to 1.5
- norm_weight: bfloat16 [1536], P(('clip', 'seq')), may hold values from 0.5 to 1.5
- norm_bias: bfloat16 [1536], P(('clip', 'seq')), may hold values from -4 to 4
- modulation: bfloat16 [6, 1536], P(None, ('clip', 'seq')), may hold values from -6 to 6
- cotangent: bfloat16 [64, 256, 1536], P('clip', 'seq'), may hold values from -6 to 6
Outputs:
- block_output: bfloat16 [64, 256, 1536], P('clip', 'seq')
- input_grad: float32 [64, 256, 1536], P('clip', 'seq')
- grad_w_qkv: float32 [1536, 4608], P(('clip', 'seq'))
- grad_attn_out: float32 [1536, 1536], P(('clip', 'seq'))
- grad_cross_q: float32 [1536, 1536], P(('clip', 'seq'))
- grad_cross_kv: float32 [1536, 3072], P(('clip', 'seq'))
- grad_cross_out: float32 [1536, 1536], P(('clip', 'seq'))
- grad_mlp_in: float32 [1536, 8960], P(('clip', 'seq'))
- grad_mlp_out: float32 [8960, 1536], P(('clip', 'seq'))
- grad_gain_q: float32 [1536], P(('clip', 'seq'))
- grad_gain_k: float32 [1536], P(('clip', 'seq'))
- grad_gain_cq: float32 [1536], P(('clip', 'seq'))
- grad_gain_ck: float32 [1536], P(('clip', 'seq'))
- grad_norm_weight: float32 [1536], P(('clip', 'seq'))
- grad_norm_bias: float32 [1536], P(('clip', 'seq'))
- grad_modulation: float32 [6, 1536], P(None, ('clip', 'seq'))
Inputs may be any that keep to these rules, and one draw needn't show every extreme that they name: positions[c, 0, t], positions[c, 1, t], positions[c, 2, t] are the frame, row and column of the grid cell of token t of clip c; the tokens of a clip take the 2 x 8 x 16 cells of a grid each once, in an order of that clip's own, and each coordinate is shifted by an offset of clip c from 0 to 15; the first clip's offsets are all 15 and the last clip's all 0.
All inputs are finite; a program needn't handle non-finite values.
Results may differ from a plain program's by a relative error of at most 0.025.
Values may be sent and summed in bfloat16 or wider, within the bound.
No kernel may reach another device: no remote copies, remote signals or barrier semaphores. Data moves between devices by JAX's collectives and lax.ppermute only.
A program may use at most 704 MiB of HBM per device.

v0:
```python
import jax
import jax.numpy as jnp
from jax import lax
from jax.sharding import PartitionSpec as P

HEADS = 12
HEAD_DIM = 128


NORM_EPS = 1e-06


def rows_first(arrays, axis, dims):
    turned = [jnp.moveaxis(a, dim, 0) for a, dim in zip(arrays, dims)]
    both = jnp.concatenate([t.reshape(len(t), -1) for t in turned], axis=1)
    whole, at, done = (lax.all_gather(both, axis, axis=0, tiled=True), 0, [])
    for t, dim in zip(turned, dims):
        share = whole[:, at : at + t[0].size].reshape(-1, *t.shape[1:])
        done.append(jnp.moveaxis(share, 0, dim))
        at += t[0].size
    return tuple(done)


def joined_along(blocks, dim):
    blocks = jnp.moveaxis(blocks, 0, dim)
    shape = blocks.shape
    return blocks.reshape(*shape[:dim], shape[dim] * shape[dim + 1], *shape[dim + 2 :])


def gather_packed(arrays, axis, dims):
    flat = jnp.concatenate([a.reshape(-1) for a in arrays])
    lines, at, done = (lax.all_gather(flat, axis), 0, [])
    for a, dim in zip(arrays, dims):
        blocks = lines[:, at : at + a.size].reshape(-1, *a.shape)
        done.append(joined_along(blocks, dim))
        at += a.size
    return tuple(done)


def split_up(array, dim, peers):
    shape = array.shape
    blocks = array.reshape(*shape[:dim], peers, shape[dim] // peers, *shape[dim + 1 :])
    return jnp.moveaxis(blocks, dim, 0)


def sum_packed(arrays, axis, dims):
    peers = lax.axis_size(axis)
    blocks = [split_up(a, dim, peers) for a, dim in zip(arrays, dims)]
    lines = jnp.concatenate([b.reshape(peers, -1) for b in blocks], axis=1)
    rows = max(16, -(-lines.shape[1] // 1024) * 8)
    lines = jnp.pad(lines, ((0, 0), (0, rows * 128 - lines.shape[1]))).reshape(-1, 128)
    flat, at, done = (lax.psum_scatter(lines, axis, tiled=True).reshape(-1), 0, [])
    for b in blocks:
        part = b[0]
        done.append(flat[at : at + part.size].reshape(part.shape))
        at += part.size
    return tuple(done)


def layer_norm(values):
    centred = values - jnp.mean(values, axis=-1, keepdims=True)
    return centred * lax.rsqrt(jnp.mean(centred * centred, axis=-1, keepdims=True) + NORM_EPS)


def rms_norm(values, gain_row):
    return (
        values * lax.rsqrt(jnp.mean(values * values, axis=-1, keepdims=True) + NORM_EPS) * gain_row
    )


def gelu_tanh(values):
    return jax.nn.gelu(values, approximate=True)


def modulated(values, shift_row, scale_row):
    return layer_norm(values) * (1.0 + scale_row) + shift_row


def affine_norm(values, weight_row, bias_row):
    return layer_norm(values) * weight_row + bias_row


def inverse_freq(pair_total):
    return 1.0 / 10000.0 ** (jnp.arange(pair_total, dtype=jnp.float32) * 2.0 / (2.0 * pair_total))


def rotary_tables(places_int, head_dim):
    pair_count = head_dim // 2
    side_pairs = pair_count // 3
    frame_pairs = pair_count - 2 * side_pairs
    places = places_int.astype(jnp.float32)
    angles = jnp.concatenate(
        [
            places[0][:, None] * inverse_freq(frame_pairs)[None, :],
            places[1][:, None] * inverse_freq(side_pairs)[None, :],
            places[2][:, None] * inverse_freq(side_pairs)[None, :],
        ],
        axis=1,
    )
    return (jnp.cos(angles), jnp.sin(angles))


def rotate(values, cos_table, sin_table):
    row_count, head_count, head_width = values.shape
    paired = values.reshape(row_count, head_count, head_width // 2, 2)
    real_part = paired[..., 0]
    imag_part = paired[..., 1]
    cos_rows = cos_table[:, None, :]
    sin_rows = sin_table[:, None, :]
    new_real = real_part * cos_rows - imag_part * sin_rows
    new_imag = real_part * sin_rows + imag_part * cos_rows
    return jnp.stack([new_real, new_imag], axis=-1).reshape(row_count, head_count, head_width)


def product(left, right):
    return jnp.dot(left, right, preferred_element_type=jnp.float32)


def inner_rows(left, right):
    return lax.dot_general(
        left, right, (((0,), (0,)), ((), ())), preferred_element_type=jnp.float32
    )


def times_transpose(left, right):
    return lax.dot_general(
        left, right, (((1,), (1,)), ((), ())), preferred_element_type=jnp.float32
    )


def score_block(query_heads, key_heads, scale_factor):
    return (
        jnp.einsum("qhd,khd->hqk", query_heads, key_heads, preferred_element_type=jnp.float32)
        * scale_factor
    )


def attend_forward(query_heads, key_heads, value_heads, scale_factor):
    scores = score_block(query_heads, key_heads, scale_factor)
    row_max = jnp.max(scores, axis=-1, keepdims=True)
    row_total = jnp.sum(jnp.exp(scores - row_max), axis=-1, keepdims=True)
    log_total = row_max + jnp.log(row_total)
    weights = jnp.exp(scores - log_total).astype(jnp.bfloat16)
    output = jnp.einsum("hqk,khd->qhd", weights, value_heads, preferred_element_type=jnp.float32)
    return (output.astype(jnp.bfloat16), log_total)


def attend_backward(query_heads, key_heads, value_heads, log_total, grad_output, scale_factor):
    scores = score_block(query_heads, key_heads, scale_factor)
    weights = jnp.exp(scores - log_total)
    weights_low = weights.astype(jnp.bfloat16)
    grad_weights = jnp.einsum(
        "qhd,khd->hqk", grad_output, value_heads, preferred_element_type=jnp.float32
    )
    delta_rows = jnp.sum(weights * grad_weights, axis=-1, keepdims=True)
    grad_scores = (weights * (grad_weights - delta_rows)).astype(jnp.bfloat16)
    grad_query = (
        jnp.einsum("hqk,khd->qhd", grad_scores, key_heads, preferred_element_type=jnp.float32)
        * scale_factor
    )
    grad_key = (
        jnp.einsum("hqk,qhd->khd", grad_scores, query_heads, preferred_element_type=jnp.float32)
        * scale_factor
    )
    grad_value = jnp.einsum(
        "hqk,qhd->khd", weights_low, grad_output, preferred_element_type=jnp.float32
    )
    return (grad_query, grad_key, grad_value)


def on_device(
    latent_tokens,
    time_embed,
    text_tokens,
    positions,
    w_qkv,
    attn_out,
    cross_q,
    cross_kv,
    cross_out,
    mlp_in,
    mlp_out,
    gain_q,
    gain_k,
    gain_cq,
    gain_ck,
    norm_weight,
    norm_bias,
    modulation,
    cotangent,
):
    attn_full = rows_first(
        (
            w_qkv,
            attn_out,
            cross_q,
            cross_kv,
            cross_out,
            gain_q,
            gain_k,
            gain_cq,
            gain_ck,
            norm_weight,
            norm_bias,
            modulation,
        ),
        ("clip", "seq"),
        (0, 0, 0, 0, 0, 0, 0, 0, 0, 0, 0, 1),
    )
    mlp_full = gather_packed((mlp_in, mlp_out), ("clip", "seq"), (0, 0))
    qkv_weight, out_weight, cq_weight, ckv_weight, co_weight = (
        attn_full[0],
        attn_full[1],
        attn_full[2],
        attn_full[3],
        attn_full[4],
    )
    gain_qf = attn_full[5].astype(jnp.float32)
    gain_kf = attn_full[6].astype(jnp.float32)
    gain_cqf = attn_full[7].astype(jnp.float32)
    gain_ckf = attn_full[8].astype(jnp.float32)
    norm_wf = attn_full[9].astype(jnp.float32)
    norm_bf = attn_full[10].astype(jnp.float32)
    in_weight, down_weight = (mlp_full[0], mlp_full[1])
    model_width = latent_tokens.shape[2]
    token_count = latent_tokens.shape[1]
    scale_factor = HEAD_DIM ** (-0.5)
    hidden = latent_tokens[0].astype(jnp.float32)
    mod_rows = time_embed[0] + attn_full[11].astype(jnp.float32)
    cos_table, sin_table = rotary_tables(positions[0], HEAD_DIM)

    def norm_rotate(query_pre, key_pre, query_gain, key_gain):
        query_rot = rotate(
            rms_norm(query_pre, query_gain).reshape(token_count, HEADS, HEAD_DIM),
            cos_table,
            sin_table,
        )
        key_rot = rotate(
            rms_norm(key_pre, key_gain).reshape(token_count, HEADS, HEAD_DIM), cos_table, sin_table
        )
        return (query_rot, key_rot)

    attn_input = modulated(hidden, mod_rows[0], mod_rows[1]).astype(jnp.bfloat16)
    qkv_pre = product(attn_input, qkv_weight)
    query_pre = qkv_pre[:, :model_width]
    key_pre = qkv_pre[:, model_width : 2 * model_width]
    value_pre = qkv_pre[:, 2 * model_width :]
    query_rot, key_rot = norm_rotate(query_pre, key_pre, gain_qf, gain_kf)
    stacked = jnp.stack(
        [query_rot, key_rot, value_pre.reshape(token_count, HEADS, HEAD_DIM)]
    ).astype(jnp.bfloat16)
    head_major = lax.all_to_all(stacked, "seq", split_axis=2, concat_axis=1, tiled=True)
    self_heads, self_lse = attend_forward(head_major[0], head_major[1], head_major[2], scale_factor)
    token_major = lax.all_to_all(self_heads, "seq", split_axis=0, concat_axis=1, tiled=True)
    attn_tokens = token_major.reshape(token_count, model_width)
    branch_one = product(attn_tokens, out_weight)
    after_attn = hidden + branch_one * mod_rows[2]
    cross_input = affine_norm(after_attn, norm_wf, norm_bf).astype(jnp.bfloat16)
    cq_pre = product(cross_input, cq_weight)
    cross_query = (
        rms_norm(cq_pre, gain_cqf).astype(jnp.bfloat16).reshape(token_count, HEADS, HEAD_DIM)
    )
    text_rows = text_tokens[0]
    ckv_pre = product(text_rows, ckv_weight)
    ck_pre = ckv_pre[:, :model_width]
    key_local = rms_norm(ck_pre, gain_ckf).astype(jnp.bfloat16)
    value_local = ckv_pre[:, model_width:].astype(jnp.bfloat16)
    text_gathered = (
        lax.all_gather(key_local, "seq", axis=0, tiled=True),
        lax.all_gather(value_local, "seq", axis=0, tiled=True),
    )
    text_total = text_gathered[0].shape[0]
    cross_key = text_gathered[0].reshape(text_total, HEADS, HEAD_DIM)
    cross_value = text_gathered[1].reshape(text_total, HEADS, HEAD_DIM)
    cross_heads, cross_lse = attend_forward(cross_query, cross_key, cross_value, scale_factor)
    cross_tokens = cross_heads.reshape(token_count, model_width)
    branch_two = product(cross_tokens, co_weight)
    after_cross = after_attn + branch_two
    mlp_input = modulated(after_cross, mod_rows[3], mod_rows[4]).astype(jnp.bfloat16)
    hidden_pre = product(mlp_input, in_weight)
    activated = gelu_tanh(hidden_pre).astype(jnp.bfloat16)
    branch_three = product(activated, down_weight)
    result = after_cross + branch_three * mod_rows[5]
    upstream = cotangent[0].astype(jnp.float32)
    grad_three = (upstream * mod_rows[5]).astype(jnp.bfloat16)
    grad_mod5 = jnp.sum(upstream * branch_three, axis=0)
    grad_mlp_out = inner_rows(activated, grad_three)
    grad_activated = times_transpose(grad_three, mlp_full[1])
    gelu_pull = jax.vjp(gelu_tanh, hidden_pre)[1]
    grad_hidden_pre = gelu_pull(grad_activated)[0].astype(jnp.bfloat16)
    grad_mlp_in = inner_rows(mlp_input, grad_hidden_pre)
    grad_mlp_input = times_transpose(grad_hidden_pre, mlp_full[0])
    mlp_norm_pull = jax.vjp(modulated, after_cross, mod_rows[3], mod_rows[4])[1]
    cross_part, grad_mod3, grad_mod4 = mlp_norm_pull(grad_mlp_input)
    grad_after_cross = upstream + cross_part
    mlp_grads = sum_packed((grad_mlp_in, grad_mlp_out), ("clip", "seq"), (0, 0))
    grad_two = grad_after_cross.astype(jnp.bfloat16)
    grad_cross_out = inner_rows(cross_tokens, grad_two)
    grad_cross_heads = (
        times_transpose(grad_two, attn_full[4])
        .astype(jnp.bfloat16)
        .reshape(token_count, HEADS, HEAD_DIM)
    )
    grad_cq_heads, grad_ck_heads, grad_cv_heads = attend_backward(
        cross_query, cross_key, cross_value, cross_lse, grad_cross_heads, scale_factor
    )
    text_grads = (
        lax.psum_scatter(
            grad_ck_heads.reshape(text_total, model_width).astype(jnp.bfloat16),
            "seq",
            scatter_dimension=0,
            tiled=True,
        ).astype(jnp.float32),
        lax.psum_scatter(
            grad_cv_heads.reshape(text_total, model_width).astype(jnp.bfloat16),
            "seq",
            scatter_dimension=0,
            tiled=True,
        ).astype(jnp.float32),
    )
    ck_pull = jax.vjp(rms_norm, ck_pre, gain_ckf)[1]
    grad_ck_pre, grad_gain_ck = ck_pull(text_grads[0])
    grad_ckv_pre = jnp.concatenate([grad_ck_pre, text_grads[1]], axis=1).astype(jnp.bfloat16)
    grad_cross_kv = inner_rows(text_rows, grad_ckv_pre)
    cq_pull = jax.vjp(rms_norm, cq_pre, gain_cqf)[1]
    grad_cq_pre, grad_gain_cq = cq_pull(grad_cq_heads.reshape(token_count, model_width))
    grad_cq_low = grad_cq_pre.astype(jnp.bfloat16)
    grad_cross_q = inner_rows(cross_input, grad_cq_low)
    grad_cross_input = times_transpose(grad_cq_low, attn_full[2])
    cross_norm_pull = jax.vjp(affine_norm, after_attn, norm_wf, norm_bf)[1]
    attn_part, grad_norm_weight, grad_norm_bias = cross_norm_pull(grad_cross_input)
    grad_after_attn = grad_after_cross + attn_part
    grad_one = (grad_after_attn * mod_rows[2]).astype(jnp.bfloat16)
    grad_mod2 = jnp.sum(grad_after_attn * branch_one, axis=0)
    grad_attn_out = inner_rows(attn_tokens, grad_one)
    grad_token_heads = (
        times_transpose(grad_one, attn_full[1])
        .astype(jnp.bfloat16)
        .reshape(token_count, HEADS, HEAD_DIM)
    )
    grad_head_major = lax.all_to_all(
        grad_token_heads, "seq", split_axis=1, concat_axis=0, tiled=True
    )
    grad_query, grad_key, grad_value = attend_backward(
        head_major[0], head_major[1], head_major[2], self_lse, grad_head_major, scale_factor
    )
    grad_stacked = lax.all_to_all(
        jnp.stack([grad_query, grad_key, grad_value]),
        "seq",
        split_axis=1,
        concat_axis=2,
        tiled=True,
    )
    rotate_pull = jax.vjp(norm_rotate, query_pre, key_pre, gain_qf, gain_kf)[1]
    grad_query_pre, grad_key_pre, grad_gain_q, grad_gain_k = rotate_pull(
        (grad_stacked[0], grad_stacked[1])
    )
    grad_qkv_pre = jnp.concatenate(
        [grad_query_pre, grad_key_pre, grad_stacked[2].reshape(token_count, model_width)], axis=1
    ).astype(jnp.bfloat16)
    grad_w_qkv = inner_rows(attn_input, grad_qkv_pre)
    grad_attn_input = times_transpose(grad_qkv_pre, attn_full[0])
    first_pull = jax.vjp(modulated, hidden, mod_rows[0], mod_rows[1])[1]
    hidden_part, grad_mod0, grad_mod1 = first_pull(grad_attn_input)
    grad_hidden = grad_after_attn + hidden_part
    grad_mod = jnp.stack([grad_mod0, grad_mod1, grad_mod2, grad_mod3, grad_mod4, grad_mod5])
    attn_grads = sum_packed(
        (
            grad_w_qkv,
            grad_attn_out,
            grad_cross_q,
            grad_cross_kv,
            grad_cross_out,
            grad_gain_q,
            grad_gain_k,
            grad_gain_cq,
            grad_gain_ck,
            grad_norm_weight,
            grad_norm_bias,
            grad_mod,
        ),
        ("clip", "seq"),
        (0, 0, 0, 0, 0, 0, 0, 0, 0, 0, 0, 1),
    )
    return (
        result.astype(jnp.bfloat16)[None],
        grad_hidden[None],
        attn_grads[0],
        attn_grads[1],
        attn_grads[2],
        attn_grads[3],
        attn_grads[4],
        mlp_grads[0],
        mlp_grads[1],
        attn_grads[5],
        attn_grads[6],
        attn_grads[7],
        attn_grads[8],
        attn_grads[9],
        attn_grads[10],
        attn_grads[11],
    )


def solution(mesh):
    placed = (
        P("clip", "seq", None),
        P("clip", None, None),
        P("clip", "seq", None),
        P("clip", None, "seq"),
        P(("clip", "seq"), None),
        P(("clip", "seq"), None),
        P(("clip", "seq"), None),
        P(("clip", "seq"), None),
        P(("clip", "seq"), None),
        P(("clip", "seq"), None),
        P(("clip", "seq"), None),
        P(("clip", "seq")),
        P(("clip", "seq")),
        P(("clip", "seq")),
        P(("clip", "seq")),
        P(("clip", "seq")),
        P(("clip", "seq")),
        P(None, ("clip", "seq")),
        P("clip", "seq", None),
    )
    return jax.shard_map(
        on_device,
        mesh=mesh,
        in_specs=placed,
        out_specs=(
            P("clip", "seq", None),
            P("clip", "seq", None),
            P(("clip", "seq"), None),
            P(("clip", "seq"), None),
            P(("clip", "seq"), None),
            P(("clip", "seq"), None),
            P(("clip", "seq"), None),
            P(("clip", "seq"), None),
            P(("clip", "seq"), None),
            P(("clip", "seq")),
            P(("clip", "seq")),
            P(("clip", "seq")),
            P(("clip", "seq")),
            P(("clip", "seq")),
            P(("clip", "seq")),
            P(None, ("clip", "seq")),
        ),
        check_vma=False,
    )
```

profile of v0, /device:TPU:1, one launch (start us, length us, event | category | flops | bytes accessed | tf_op | source)
XLA Modules:
  0.0 2673.0 jit_solution(15405517303451293681)
XLA Ops:
  14.5 373.1 %all-gather.13.cloned.1.call-done = bf16[128,12,12300]{2,1,0:T(8,128)(2,1)} async-done(((bf16[1,12,12300]{2,1,0:T(8,128)(2,1)}), bf16[128,12,12300]{2,1,0:T(8,128)(2,1)}) %all-gather.13.cloned.1.call-update) | async-done | bytes 37785616 | tf_op jit(solution)/shard_map/all_gather | solution.py:16
  387.6 55.5 %reshape.585 = bf16[1536,12300]{1,0:T(8,128)(2,1)} reshape(bf16[128,12,12300]{2,1,0:T(8,128)(2,1)} %all-gather.13.cloned.1.call-done) | data formatting | bytes 75571200
  485.4 17.9 all_to_all.63
  507.8 15.6 all_to_all.64
  545.4 357.9 %all-gather.11.cloned.1.call-done = bf16[27525120]{0:T(1024)(128)(2,1)} async-done(((bf16[215040]{0:T(1024)(128)(2,1)}), bf16[27525120]{0:T(1024)(128)(2,1)}) %all-gather.11.cloned.1.call-update) | async-done | bytes 55050256 | tf_op jit(solution)/shard_map/all_gather | solution.py:32
  903.3 47.9 %reshape.583 = bf16[128,215040]{1,0:T(8,128)(2,1)} reshape(bf16[27525120]{0:T(1024)(128)(2,1)} %all-gather.11.cloned.1.call-done) | data formatting | bytes 110100480 | tf_op jit(solution)/shard_map/all_gather | solution.py:32
  951.3 36.0 %fusion.118 = (bf16[128,107520]{1,0:T(8,128)(2,1)}, bf16[128,107520]{1,0:T(8,128)(2,1)}) fusion(bf16[128,215040]{1,0:T(8,128)(2,1)} %reshape.583), kind=kLoop, calls=%fused_computation.244 | loop fusion | bytes 110100480 | tf_op jit(solution)/shard_map/slice | solution.py:34
  987.2 44.0 %reshape_reshape.35 = bf16[1536,8960]{1,0:T(8,128)(2,1)} reshape(bf16[128,107520]{1,0:T(8,128)(2,1)} %get-tuple-element.62) | data formatting | bytes 55050240 | tf_op jit(solution)/shard_map/reshape;reshape | solution.py:27
  1031.3 44.4 %reshape_reshape.36 = bf16[8960,1536]{1,0:T(8,128)(2,1)} reshape(bf16[128,107520]{1,0:T(8,128)(2,1)} %get-tuple-element.63) | data formatting | bytes 55050240 | tf_op jit(solution)/shard_map/reshape;reshape | solution.py:27
  1075.7 11.0 fusion.112
  1088.9 15.3 fusion.12
  1104.2 15.5 multiply_reduce_fusion.4
  1119.8 15.9 fusion.66
  1182.5 11.8 reshape_reshape.39
  1209.8 11.7 reshape_reshape.38
  1226.5 11.7 reshape_reshape.41
  1269.1 11.6 fusion.77
  1282.4 29.9 %reshape_reshape.37 = f32[128,55296]{1,0:T(8,128)} reshape(f32[1536,4608]{1,0:T(8,128)} %fusion.77) | data formatting | bytes 56623104 | tf_op jit(solution)/shard_map/reshape;reshape | solution.py:49
  1312.3 19.8 constant_dynamic-update-slice_fusion.10
  1362.4 18.7 copy.245
  1381.1 22.4 reshape_reshape.40
  1403.5 12.5 constant_dynamic-update-slice_fusion.7
  1436.1 49.6 %pad.20 = f32[128,148480]{1,0:T(8,128)} pad(f32[128,147600]{1,0:T(8,128)} %dynamic-update-slice.11, f32[]{:T(128)} %constant.26.clone.1), padding=0_0x0_880 | pad | bytes 151592960 | tf_op jit(solution)/shard_map/jit(_pad)/pad | solution.py:51
  1485.8 83.2 %reshape.565 = f32[148480,128]{1,0:T(8,128)} reshape(f32[128,148480]{1,0:T(8,128)} %pad.20) | data formatting | bytes 152043520 | tf_op jit(solution)/shard_map/reshape | solution.py:51
  1570.0 27.4 %fusion.84 = f32[8960,1536]{1,0:T(8,128)} fusion(bf16[1,128,1536]{2,1,0:T(8,128)(2,1)S(1)} %copy-done.32, f32[1536]{0:T(1024)S(1)} %copy-done.88, f32[128,8960]{1,0:T(8,128)} %copy-done.8), kind=kOutput, calls=%fused_computation.159 | convolution fusion | flops 3534127104 | bytes 60037120 | tf_op jit(solution)/shard_map/dot_general | solution.py:120
  1597.5 52.1 %reshape_reshape.43 = f32[128,107520]{1,0:T(8,128)} reshape(f32[8960,1536]{1,0:T(8,128)} %fusion.84) | data formatting | bytes 110100480 | tf_op jit(solution)/shard_map/reshape;reshape | solution.py:49
  1649.6 24.0 fusion.111
  1673.6 46.8 %reshape_reshape.42 = f32[128,107520]{1,0:T(8,128)} reshape(f32[1536,8960]{1,0:T(8,128)} %fusion.111) | data formatting | bytes 110100480 | tf_op jit(solution)/shard_map/reshape;reshape | solution.py:49
  1720.4 75.5 %pad_maximum_fusion = f32[128,215040]{1,0:T(8,128)} fusion(f32[128,107520]{1,0:T(8,128)} %reshape_reshape.43, f32[128,107520]{1,0:T(8,128)} %reshape_reshape.42), kind=kLoop, calls=%fused_computation | loop fusion | flops 27525120 | bytes 220200960 | tf_op jit(solution)/shard_map/concatenate | solution.py:49
  1795.8 112.8 %reshape.571 = f32[215040,128]{1,0:T(8,128)} reshape(f32[128,215040]{1,0:T(8,128)} %pad_maximum_fusion) | data formatting | bytes 220200960 | tf_op jit(solution)/shard_map/reshape | solution.py:51
  1911.4 125.5 %all-reduce.10.cloned.1.call-done = f32[148480,128]{1,0:T(8,128)} async-done(((f32[148480,128]{1,0:T(8,128)}), f32[148480,128]{1,0:T(8,128)}) %all-reduce.10.cloned.1.call-update) | async-done | bytes 76021776
  2045.6 617.4 %all-reduce.12.cloned.1.call-done = f32[215040,128]{1,0:T(8,128)} async-done(((f32[215040,128]{1,0:T(8,128)}), f32[215040,128]{1,0:T(8,128)}) %all-reduce.12.cloned.1.call-update) | async-done | bytes 110100496
  (488 shorter events, 242.5 us)
Async XLA Ops:
  7.2 440.3 %copy-start = (bf16[1,256,1536]{2,1,0:T(8,128)(2,1)S(1)}, bf16[1,256,1536]{2,1,0:T(8,128)(2,1)}, u32[]{:S(2)}) copy-start(bf16[1,256,1536]{2,1,0:T(8,128)(2,1)} %param.21) | copy-start | bytes 2359300
  7.2 380.4 %all-gather.13.cloned.1.call-start = ((), (), s32[]{:S(2)}) async-start(), calls=%async_computation.11 | async-start | bytes 51253248 | tf_op jit(solution)/shard_map/all_gather | solution.py:16
  14.5 518.9 %all-gather.9.cloned.1.call-start = ((), (), s32[]{:S(2)}) async-start(), calls=%async_computation.7 | async-start | bytes 2359296 | tf_op jit(solution)/shard_map/all_gather | solution.py:269
  455.6 82.8 %all-gather.7.cloned.1.call-start = ((), (), s32[]{:S(2)}) async-start(), calls=%async_computation.6 | async-start | bytes 2359296 | tf_op jit(solution)/shard_map/all_gather | solution.py:270
  458.7 444.6 %all-gather.11.cloned.1.call-start = ((), (), s32[]{:S(2)}) async-start(), calls=%async_computation.10 | async-start | bytes 55480320 | tf_op jit(solution)/shard_map/all_gather | solution.py:32
  459.5 889.0 %reduce-scatter.3.cloned.1.call-start = ((), (), s32[]{:S(2)}) async-start(), calls=%async_computation.8 | async-start | bytes 2359296 | tf_op jit(solution)/shard_map/reduce_scatter | solution.py:308
  465.2 610.5 %copy-start.55 = (f32[1536]{0:T(1024)}, f32[1536]{0:T(1024)S(1)}, u32[]{:S(2)}) copy-start(f32[1536]{0:T(1024)S(1)} %get-tuple-element.44) | copy-start | bytes 18436
  465.2 654.6 %copy-start.53 = (f32[1536]{0:T(1024)}, f32[1536]{0:T(1024)S(1)}, u32[]{:S(2)}) copy-start(f32[1536]{0:T(1024)S(1)} %get-tuple-element.45) | copy-start | bytes 18436
  505.3 18.5 copy-start.80
  528.0 13.7 copy-start.6
  545.1 574.7 %copy-start.9 = (f32[128,1536]{1,0:T(8,128)}, f32[128,1536]{1,0:T(8,128)S(1)}, u32[]{:S(2)}) copy-start(f32[128,1536]{1,0:T(8,128)S(1)} %get-tuple-element.110) | copy-start | bytes 2359300
  545.1 559.1 %copy-start.99 = (f32[128]{0:T(128)}, f32[128]{0:T(128)S(1)}, u32[]{:S(2)}) copy-start(f32[128]{0:T(128)S(1)} %broadcast_multiply_fusion.3) | copy-start | bytes 1540
  545.4 558.8 %copy-start.104 = (f32[128]{0:T(128)}, f32[128]{0:T(128)S(1)}, u32[]{:S(2)}) copy-start(f32[128]{0:T(128)S(1)} %fusion.101) | copy-start | bytes 1540
  1075.7 13.2 copy-start.31
  1075.7 13.2 copy-start.86
  1104.2 15.6 copy-start.87
  1168.0 26.3 all-to-all-start.2
  1199.3 42.8 %all-to-all-start.3 = ((f32[3,256,6,128]{3,2,0,1:T(8,128)}), f32[3,256,6,128]{3,2,0,1:T(8,128)}, u32[]{:S(2)}, u32[]{:S(2)}) async-start(f32[3,256,6,128]{3,2,0,1:T(8,128)} %copy.237), calls=%async_computation.3 | async-start | bytes 6291456 | tf_op jit(solution)/shard_map/all_to_all | solution.py:347
  1204.7 148.5 %reduce-scatter.5.cloned.1.call-start = ((), (), s32[]{:S(2)}) async-start(), calls=%async_computation.9 | async-start | bytes 2359296 | tf_op jit(solution)/shard_map/reduce_scatter | solution.py:314
  1242.1 794.8 %all-reduce.10.cloned.1.call-start = ((), (), s32[]{:S(2)}) async-start(), calls=%async_computation.12 | async-start | bytes 152043520
  1269.1 13.1 copy-start.93
  1269.1 13.2 copy-start.89
  1416.0 14.9 copy-start.62
  1416.0 16.7 copy-start.61
  1569.0 1094.0 %all-reduce.12.cloned.1.call-start = ((), (), s32[]{:S(2)}) async-start(), calls=%async_computation.13 | async-start | bytes 220200960
  1597.4 52.2 %copy-start.10 = (f32[128,1536]{1,0:T(8,128)S(1)}, f32[128,1536]{1,0:T(8,128)}, u32[]{:S(2)}) copy-start(f32[128,1536]{1,0:T(8,128)} %copy-done.9) | copy-start | bytes 2359300
  1597.4 52.2 %copy-start.14 = (bf16[128,8960]{1,0:T(8,128)(2,1)S(1)}, bf16[128,8960]{1,0:T(8,128)(2,1)}, u32[]{:S(2)}) copy-start(bf16[128,8960]{1,0:T(8,128)(2,1)} %fusion.12) | copy-start | bytes 6881284
  1597.4 52.2 %copy-start.54 = (f32[1536]{0:T(1024)S(1)}, f32[1536]{0:T(1024)}, u32[]{:S(2)}) copy-start(f32[1536]{0:T(1024)} %copy-done.53) | copy-start | bytes 18436
  1597.4 52.2 %copy-start.56 = (f32[1536]{0:T(1024)S(1)}, f32[1536]{0:T(1024)}, u32[]{:S(2)}) copy-start(f32[1536]{0:T(1024)} %copy-done.55) | copy-start | bytes 18436
  1597.4 52.2 %copy-start.100 = (f32[128]{0:T(128)S(1)}, f32[128]{0:T(128)}, u32[]{:S(2)}) copy-start(f32[128]{0:T(128)} %copy-done.99) | copy-start | bytes 1540
  1597.4 52.2 %copy-start.105 = (f32[128]{0:T(128)S(1)}, f32[128]{0:T(128)}, u32[]{:S(2)}) copy-start(f32[128]{0:T(128)} %copy-done.104) | copy-start | bytes 1540
  2039.5 626.4 %copy-start.1 = (bf16[1,256,1536]{2,1,0:T(8,128)(2,1)S(1)}, bf16[1,256,1536]{2,1,0:T(8,128)(2,1)}, u32[]{:S(2)}) copy-start(bf16[1,256,1536]{2,1,0:T(8,128)(2,1)} %param.21) | copy-start | bytes 2359300
  (120 other events, 578.7 us)
Sparse Core Ops, SparseCore 0:
  14.6 372.9 all-gather.12
  455.7 30.2 all-gather.8
  487.6 37.8 all-gather.6
  527.6 375.6 all-gather.10
  1152.9 33.3 reduce-scatter.2
  1242.2 29.5 reduce-scatter.4
  1569.2 467.6 all-reduce.9
  2043.8 619.1 all-reduce.11
where the time goes:
time: 2690 us; the launch traced here: 2670 us
  waiting for transfers between devices  1470 us (55%)
  local copies, waits for them, and re-layouts  813 us (30%)
  matrix products  208 us (8%)
  other arithmetic  119 us (4%)
  blocking collectives  33.4 us (1%)
    unnamed x10, waiting for transfers between devices  743 us
    all_gather x1, waiting for transfers between devices, rows_first(): whole, at, done = (lax.all_gather(both, axis, axis=0, tiled=True), 0, [])  373 us
    all_gather x1, waiting for transfers between devices, gather_packed(): lines, at, done = (lax.all_gather(flat, axis), 0, [])  358 us
    reshape x2, local copies, waits for them, and re-layouts, sum_packed(): jnp.pad(lines, ((0, 0), (0, rows * 128 - lines.shape[1]))).reshape(-1, 128)  196 us
    another operation x7, local copies, waits for them, and re-layouts, sum_packed(): lines = jnp.concatenate([b.reshape(peers, -1) for b in blocks], axis=1)  186 us
    unnamed x303, local copies, waits for them, and re-layouts  138 us
    another operation x2, local copies, waits for them, and re-layouts, joined_along(): blocks.reshape(*shape[:dim], shape[dim] * shape[dim + 1], *shape[dim + 2:])  88.5 us
    dot_general x7, matrix products, inner_rows(): lax.dot_general(left, right, (((0,), (0,)), ((), ())), preferred_element_...  87.5 us
  transfers between devices with their start and end apart: 10, of which 4 were waited for; matrix products, arithmetic and copies ran while one was open for 22% of the time, Pallas kernels for 0%

commit v1 on v0

v1 whole, which is shorter than its diff:
```python
import functools

import jax
import jax.numpy as jnp
from jax import lax
from jax.experimental import pallas as pl
from jax.experimental.pallas import tpu as pltpu
from jax.sharding import Mesh
from jax.sharding import PartitionSpec as P

HEADS = 12
HEAD_DIM = 128
NORM_EPS = 1e-06
SCALE = HEAD_DIM ** (-0.5)

bf16 = jnp.bfloat16
f32 = jnp.float32

GROUP = ("core", "zl")
CHIPS = ("zh", "zl")
LINE = ("zh", "core", "zl")
PLACES = ("y", "x")
SWAP = [(0, 1), (1, 0)]
CROSS = [(0, 3), (3, 0), (1, 2), (2, 1)]


def mm(left, right):
    return jnp.dot(left, right, preferred_element_type=f32)


def mm_tn(left, right):
    return lax.dot_general(left, right, (((0,), (0,)), ((), ())), preferred_element_type=f32)


def mm_nt(left, right):
    return lax.dot_general(left, right, (((1,), (1,)), ((), ())), preferred_element_type=f32)


def swap(array, axis_name):
    return lax.ppermute(array, axis_name, SWAP)


def others(array, axis_name):
    size = lax.axis_size(axis_name)
    return [array] + [
        lax.ppermute(array, axis_name, [(i, i ^ k) for i in range(size)]) for k in range(1, size)
    ]


def in_order(parts, index):
    step = 1
    parts = list(parts)
    while step < len(parts):
        turned = index // step % 2 == 1
        for k in range(len(parts)):
            if k & step == 0:
                low, high = parts[k], parts[k + step]
                parts[k], parts[k + step] = jnp.where(turned, high, low), jnp.where(turned, low, high)
        step *= 2
    return parts


def axis_join(piece, axis_name, dim=0):
    return jnp.concatenate(in_order(others(piece, axis_name), lax.axis_index(axis_name)), dim)


def near_sum(blocks, axis_name):
    size = lax.axis_size(axis_name)
    total = blocks[0].astype(f32)
    for k in range(1, size):
        pairs = [(i, i ^ k) for i in range(size)]
        total = total + lax.ppermute(blocks[k], axis_name, pairs).astype(f32)
    return total


def group_sum(small):
    return (
        small + swap(small, "zl") + swap(small, "core") + lax.ppermute(small, GROUP, CROSS)
    )


def core_sum(small):
    return small + swap(small, "core")


def ordered(mine, other, axis_name, dim):
    first = lax.axis_index(axis_name) == 0
    return jnp.where(
        first, jnp.concatenate([mine, other], dim), jnp.concatenate([other, mine], dim)
    )


def join(piece, axis_name, dim):
    return ordered(piece, swap(piece, axis_name), axis_name, dim)


def halves(whole, axis_name, dim):
    low, high = jnp.split(whole, 2, dim)
    first = lax.axis_index(axis_name) == 0
    return jnp.where(first, low, high), jnp.where(first, high, low)


def trade(whole, axis_name, cut, lay):
    keep, give = halves(whole, axis_name, cut)
    return ordered(keep, swap(give, axis_name), axis_name, lay)


def scatter_sum(partial, axis_name, dim):
    keep, give = halves(partial, axis_name, dim)
    return keep.astype(f32) + swap(give.astype(bf16), axis_name).astype(f32)


def by_seq(rows):
    return rows.reshape(2, rows.shape[0] // 2, rows.shape[1])


def flat(rows):
    return rows.reshape(-1, rows.shape[-1])


def layer_norm(values):
    centred = values - jnp.mean(values, axis=-1, keepdims=True)
    inv = lax.rsqrt(jnp.mean(centred * centred, axis=-1, keepdims=True) + NORM_EPS)
    return centred * inv, inv


def split_norm(values):
    local = values.shape[1]
    mean_here = jnp.mean(values, axis=-1)
    centred = values - mean_here[:, None]
    mine = jnp.stack([mean_here, jnp.sum(centred * centred, axis=-1)])
    other = swap(mine, "core")
    mean = (mine[0] + other[0]) / 2
    apart = mine[0] - mean
    spread = mine[1] + other[1] + 2 * local * apart * apart
    inv = lax.rsqrt(spread / (2 * local) + NORM_EPS)
    return (values - mean[:, None]) * inv[:, None], inv


def turn(values, cos, sin):
    lanes = lax.broadcasted_iota(jnp.int32, values.shape, 1)
    swapped = jnp.where(
        lanes % 2 == 0,
        -pltpu.roll(values, HEAD_DIM - 1, 1),
        pltpu.roll(values, 1, 1),
    )
    return values * cos + swapped * sin


def attend(query, key):
    scores = mm_nt(query, key) * SCALE
    peak = jnp.max(scores, axis=-1, keepdims=True)
    weights = jnp.exp(scores - peak)
    weights = weights / jnp.sum(weights, axis=-1, keepdims=True)
    return weights


def attend_grads(query, key, value, grad):
    weights = attend(query, key)
    grad_weights = mm_nt(grad, value)
    delta = jnp.sum(weights * grad_weights, axis=-1, keepdims=True)
    grad_scores = (weights * (grad_weights - delta)).astype(bf16)
    grad_query = mm(grad_scores, key) * SCALE
    grad_key = mm_tn(grad_scores, query) * SCALE
    grad_value = mm_tn(weights.astype(bf16), grad)
    return grad_query, grad_key, grad_value


def self_forward_kernel(q_ref, k_ref, v_ref, r_ref, gq_ref, gk_ref, cos_ref, sin_ref,
                        qr_ref, kr_ref, vb_ref, o_ref):
    cos, sin = cos_ref[...], sin_ref[...]
    query = turn(q_ref[...] * r_ref[:, 0:1] * gq_ref[...], cos, sin).astype(bf16)
    key = turn(k_ref[...] * r_ref[:, 1:2] * gk_ref[...], cos, sin).astype(bf16)
    value = v_ref[...].astype(bf16)
    qr_ref[...] = query
    kr_ref[...] = key
    vb_ref[...] = value
    weights = attend(query, key).astype(bf16)
    o_ref[...] = mm(weights, value).astype(bf16)


def self_forward(qkv, inverse, gain_q, gain_k, cos, sin, clips):
    rows, local = qkv.shape[0], qkv.shape[1] // 3
    heads, tokens = local // HEAD_DIM, rows // clips

    def at(shift):
        return pl.BlockSpec((tokens, HEAD_DIM), lambda b, h, s=shift: (b, h + s))

    gain = pl.BlockSpec((1, HEAD_DIM), lambda b, h: (0, h))
    table = pl.BlockSpec((tokens, HEAD_DIM), lambda b, h: (b, 0))
    return pl.pallas_call(
        self_forward_kernel,
        grid=(clips, heads),
        in_specs=[at(0), at(heads), at(2 * heads),
                  pl.BlockSpec((tokens, 2), lambda b, h: (b, 0)), gain, gain, table, table],
        out_specs=[at(0)] * 4,
        out_shape=[jax.ShapeDtypeStruct((rows, local), bf16)] * 4,
        cost_estimate=pl.CostEstimate(flops=8 * 10**9, bytes_accessed=10**7, transcendentals=10**6),
        name="self_forward",
    )(qkv, qkv, qkv, inverse, gain_q, gain_k, cos, sin)


def self_backward_kernel(qr_ref, kr_ref, vb_ref, do_ref, q_ref, k_ref, r_ref, gq_ref, gk_ref,
                         cos_ref, sin_ref, uq_ref, uk_ref, dv_ref, part_ref, dgain_ref):
    cos, sin = cos_ref[...], sin_ref[...]
    grad_query, grad_key, grad_value = attend_grads(
        qr_ref[...], kr_ref[...], vb_ref[...], do_ref[...]
    )
    up_q = turn(grad_query, cos, -sin)
    up_k = turn(grad_key, cos, -sin)
    dv_ref[...] = grad_value.astype(bf16)
    vq, vk = up_q * q_ref[...], up_k * k_ref[...]
    dgain_ref[0, 0, 0:1, :] = jnp.sum(vq * r_ref[:, 0:1], axis=0, keepdims=True)
    dgain_ref[0, 0, 1:2, :] = jnp.sum(vk * r_ref[:, 1:2], axis=0, keepdims=True)
    up_q, up_k = up_q * gq_ref[...], up_k * gk_ref[...]
    uq_ref[...] = up_q
    uk_ref[...] = up_k
    mean_q = jnp.sum(vq * gq_ref[...], axis=-1, keepdims=True)
    mean_k = jnp.sum(vk * gk_ref[...], axis=-1, keepdims=True)
    both = jnp.concatenate([mean_q, mean_k], axis=1)

    @pl.when(pl.program_id(1) == 0)
    def _():
        part_ref[...] = both

    @pl.when(pl.program_id(1) > 0)
    def _():
        part_ref[...] += both


def self_backward(qr, kr, vb, grad, qkv, inverse, gain_q, gain_k, cos, sin, clips):
    rows, local = qr.shape
    heads, tokens = local // HEAD_DIM, rows // clips

    def at(shift):
        return pl.BlockSpec((tokens, HEAD_DIM), lambda b, h, s=shift: (b, h + s))

    gain = pl.BlockSpec((1, HEAD_DIM), lambda b, h: (0, h))
    table = pl.BlockSpec((tokens, HEAD_DIM), lambda b, h: (b, 0))
    pair = pl.BlockSpec((tokens, 2), lambda b, h: (b, 0))
    return pl.pallas_call(
        self_backward_kernel,
        grid=(clips, heads),
        in_specs=[at(0)] * 4 + [at(0), at(heads), pair, gain, gain, table, table],
        out_specs=[at(0)] * 3 + [pair, pl.BlockSpec((1, 1, 2, HEAD_DIM), lambda b, h: (b, h, 0, 0))],
        out_shape=[
            jax.ShapeDtypeStruct((rows, local), f32),
            jax.ShapeDtypeStruct((rows, local), f32),
            jax.ShapeDtypeStruct((rows, local), bf16),
            jax.ShapeDtypeStruct((rows, 2), f32),
            jax.ShapeDtypeStruct((clips, heads, 2, HEAD_DIM), f32),
        ],
        cost_estimate=pl.CostEstimate(flops=11 * 10**9, bytes_accessed=10**7, transcendentals=10**6),
        name="self_backward",
    )(qr, kr, vb, grad, qkv, qkv, inverse, gain_q, gain_k, cos, sin)


def cross_forward_kernel(q_ref, r_ref, g_ref, k_ref, v_ref, qn_ref, o_ref):
    tokens, words = q_ref.shape[0] // 2, k_ref.shape[0] // 2
    for clip in range(2):
        rows, text = pl.ds(clip * tokens, tokens), pl.ds(clip * words, words)
        query = (q_ref[rows, :] * r_ref[rows, :] * g_ref[...]).astype(bf16)
        qn_ref[rows, :] = query
        weights = attend(query, k_ref[text, :]).astype(bf16)
        o_ref[rows, :] = mm(weights, v_ref[text, :]).astype(bf16)


def cross_forward(cq, inverse, gain, key, value):
    rows, local = cq.shape
    at = pl.BlockSpec((rows, HEAD_DIM), lambda h: (0, h))
    text = pl.BlockSpec((key.shape[0], HEAD_DIM), lambda h: (0, h))
    return pl.pallas_call(
        cross_forward_kernel,
        grid=(local // HEAD_DIM,),
        in_specs=[at, pl.BlockSpec((rows, 1), lambda h: (0, 0)),
                  pl.BlockSpec((1, HEAD_DIM), lambda h: (0, h)), text, text],
        out_specs=[at, at],
        out_shape=[jax.ShapeDtypeStruct((rows, local), bf16)] * 2,
        cost_estimate=pl.CostEstimate(flops=9 * 10**9, bytes_accessed=10**7, transcendentals=10**6),
        name="cross_forward",
    )(cq, inverse, gain, key, value)


def cross_backward_kernel(qn_ref, k_ref, v_ref, do_ref, dq_ref, dk_ref, dv_ref):
    tokens, words = qn_ref.shape[0] // 2, k_ref.shape[0] // 2
    for clip in range(2):
        rows, text = pl.ds(clip * tokens, tokens), pl.ds(clip * words, words)
        grad_query, grad_key, grad_value = attend_grads(
            qn_ref[rows, :], k_ref[text, :], v_ref[text, :], do_ref[rows, :]
        )
        dq_ref[rows, :] = grad_query
        dk_ref[text, :] = grad_key
        dv_ref[text, :] = grad_value.astype(bf16)


def cross_backward(query, key, value, grad):
    rows, local = query.shape
    at = pl.BlockSpec((rows, HEAD_DIM), lambda h: (0, h))
    text = pl.BlockSpec((key.shape[0], HEAD_DIM), lambda h: (0, h))
    return pl.pallas_call(
        cross_backward_kernel,
        grid=(local // HEAD_DIM,),
        in_specs=[at, text, text, at],
        out_specs=[at, text, text],
        out_shape=[
            jax.ShapeDtypeStruct((rows, local), f32),
            jax.ShapeDtypeStruct(key.shape, f32),
            jax.ShapeDtypeStruct(key.shape, bf16),
        ],
        cost_estimate=pl.CostEstimate(flops=11 * 10**9, bytes_accessed=10**7, transcendentals=10**6),
        name="cross_backward",
    )(query, key, value, grad)


PACK = 256
REST = 768
GELU_A = 0.7978845608028654
GELU_B = 0.044715


def mlp_kernel(core_ref, x_ref, xo_ref, g_ref, go_ref, pack_ref, act_ref, gh_ref, gx_ref, gxo_ref,
               up, down, act, gh, total, total_other, sems, out_sems):
    peers, up_rows, hidden = up.shape
    down_rows, width = down.shape[1:]
    half = width // 2
    cuts = [0, hidden // PACK // 2 * PACK, hidden]
    loads, last = [], 0
    for k in range(2):
        first, last = last, -(-cuts[k + 1] // down_rows)
        moves = [
            (pack_ref.at[:, pl.ds(at // PACK * up_rows, up_rows), :], up.at[:, :, pl.ds(at, PACK)])
            for at in range(cuts[k], cuts[k + 1], PACK)
        ]
        for at in range(0, width, PACK):
            line = hidden // PACK * up_rows + at // PACK * down_rows
            moves.append(
                (
                    pack_ref.at[pl.ds(first, last - first), pl.ds(line, down_rows), :],
                    down.at[pl.ds(first, last - first), :, pl.ds(at, PACK)],
                )
            )
        loads.append([pltpu.make_async_copy(*m, sems.at[k, i]) for i, m in enumerate(moves)])
        for copy in loads[-1]:
            copy.start()
    down_flat = down.reshape(peers * down_rows, width)
    up_flat = up.reshape(peers * up_rows, hidden)
    mine = pl.ds(pl.multiple_of(core_ref[0] * half, half), half)
    other = pl.ds(pl.multiple_of((1 - core_ref[0]) * half, half), half)
    stores = []
    for k in range(2):
        for copy in loads[k]:
            copy.wait()
        cols = pl.ds(cuts[k], cuts[k + 1] - cuts[k])
        pre = mm(x_ref[...], up_flat[mine, cols]) + mm(xo_ref[...], up_flat[other, cols])
        grad = mm_nt(g_ref[...], down_flat[cols, mine]) + mm_nt(go_ref[...], down_flat[cols, other])
        square = pre * pre
        tanh = jnp.tanh(GELU_A * pre * (1.0 + GELU_B * square))
        share = 0.5 * (1.0 + tanh)
        act[:, cols] = (pre * share).astype(bf16)
        slope = share + pre * (0.5 * GELU_A) * (1.0 - tanh * tanh) * (1.0 + 3 * GELU_B * square)
        grad = (grad * slope).astype(bf16)
        gh[:, cols] = grad
        for i, (here, there) in enumerate(((act, act_ref), (gh, gh_ref))):
            stores.append(pltpu.make_async_copy(here.at[:, cols], there.at[:, cols], out_sems.at[k, i]))
            stores[-1].start()
        for rows, sums, out in ((mine, total, gx_ref), (other, total_other, gxo_ref)):
            part = mm_nt(grad, up_flat[rows, cols])
            if k == 0:
                sums[...] = part
            else:
                out[...] = (sums[...] + part).astype(bf16)
    for copy in stores:
        copy.wait()


def mlp(core, inputs, grads, packed, up_rows, hidden, down_rows):
    rows, half = inputs[0].shape
    width = 2 * half
    peers = packed.shape[0]
    copies = -(-hidden // PACK // 2) + width // PACK
    vmem = pl.BlockSpec(memory_space=pltpu.VMEM)
    any_space = pl.BlockSpec(memory_space=pl.ANY)
    return pl.pallas_call(
        mlp_kernel,
        in_specs=[pl.BlockSpec(memory_space=pltpu.SMEM)] + [vmem] * 4 + [any_space],
        out_specs=[any_space, any_space, vmem, vmem],
        out_shape=[
            jax.ShapeDtypeStruct((rows, hidden), bf16),
            jax.ShapeDtypeStruct((rows, hidden), bf16),
            jax.ShapeDtypeStruct((rows, half), bf16),
            jax.ShapeDtypeStruct((rows, half), bf16),
        ],
        scratch_shapes=[
            pltpu.VMEM((peers, up_rows, hidden), bf16),
            pltpu.VMEM((peers, down_rows, width), bf16),
            pltpu.VMEM((rows, hidden), bf16),
            pltpu.VMEM((rows, hidden), bf16),
            pltpu.VMEM((rows, half), f32),
            pltpu.VMEM((rows, half), f32),
            pltpu.SemaphoreType.DMA((2, copies)),
            pltpu.SemaphoreType.DMA((2, 2)),
        ],
        compiler_params=pltpu.CompilerParams(vmem_limit_bytes=56 * 2**20),
        cost_estimate=pl.CostEstimate(
            flops=6 * rows * width * hidden, bytes_accessed=packed.size * 2, transcendentals=rows * hidden
        ),
        name="mlp",
    )(core, *inputs, *grads, packed)


def tn_pack_kernel(place, x_ref, g_ref, *rest):
    pack_ref, held, sems = rest[-3:]
    peers, rows, _ = held.shape[1:]
    slots = held.shape[0]
    copies = []
    for k in range(slots):
        grad = g_ref[:, k * REST : (k + 1) * REST]
        lines = held.at[k].reshape(peers * rows, REST)
        lines[...] = mm_tn(x_ref[...], grad).astype(bf16)
        copies.append(
            pltpu.make_async_copy(
                held.at[k], pack_ref.at[:, pl.ds((place + k) * rows, rows), :], sems.at[k]
            )
        )
        copies[-1].start()
    for copy in copies:
        copy.wait()


def tn_pack(left, right, place, places, peers, packed=None):
    width, slots = left.shape[1], right.shape[1] // REST
    rows = width // peers
    vmem = pl.BlockSpec(memory_space=pltpu.VMEM)
    any_space = pl.BlockSpec(memory_space=pl.ANY)
    given = [] if packed is None else [packed]
    return pl.pallas_call(
        functools.partial(tn_pack_kernel, place),
        in_specs=[vmem, vmem] + [any_space] * len(given),
        out_specs=any_space,
        out_shape=jax.ShapeDtypeStruct((peers, places * rows, REST), bf16),
        scratch_shapes=[pltpu.VMEM((slots, peers, rows, REST), bf16), pltpu.SemaphoreType.DMA((slots,))],
        input_output_aliases={2: 0} if given else {},
        compiler_params=pltpu.CompilerParams(vmem_limit_bytes=56 * 2**20),
        cost_estimate=pl.CostEstimate(
            flops=2 * left.size * right.shape[1], bytes_accessed=2 * width * right.shape[1], transcendentals=0
        ),
        name="tn_pack",
    )(left, right, *given)


def mlp_grads_kernel(core_ref, x_ref, xo_ref, gh_ref, act_ref, g_ref, go_ref, pack_ref, up, down, up_sems, down_sems):
    copies = []
    blocks, peers, rows, _ = up.shape
    some = peers // 2
    line = blocks * rows
    for part, left in enumerate((x_ref, xo_ref)):
        first = core_ref[0] if part == 0 else 1 - core_ref[0]
        grad = mm_tn(left[...], gh_ref[...]).astype(bf16)
        for k in range(blocks):
            held = up.at[k, pl.ds(part * some, some)]
            held[...] = grad[:, k * PACK : (k + 1) * PACK].reshape(some, rows, PACK)
            there = pack_ref.at[pl.ds(first * some, some), pl.ds(k * rows, rows), :]
            copies.append(pltpu.make_async_copy(held, there, up_sems.at[part, k]))
            copies[-1].start()
    blocks, _, rows, _ = down.shape
    for part, right in enumerate((g_ref, go_ref)):
        first = core_ref[0] if part == 0 else 1 - core_ref[0]
        grad = mm_tn(act_ref[...], right[...]).astype(bf16)
        for k in range(blocks // 2):
            held = down.at[part * (blocks // 2) + k]
            held[...] = grad[:, k * PACK : (k + 1) * PACK].reshape(peers, rows, PACK)
            at = pl.multiple_of(line + (first * (blocks // 2) + k) * rows, 16)
            there = pack_ref.at[:, pl.ds(at, rows), :]
            copies.append(pltpu.make_async_copy(held, there, down_sems.at[part, k]))
            copies[-1].start()
    for copy in copies:
        copy.wait()


def mlp_grads(core, inputs, grad_hidden, activated, grads, peers):
    width, hidden = 2 * inputs[0].shape[1], activated.shape[1]
    up_rows, down_rows = width // peers, hidden // peers
    lines = hidden // PACK * up_rows + width // PACK * down_rows
    vmem = pl.BlockSpec(memory_space=pltpu.VMEM)
    return pl.pallas_call(
        mlp_grads_kernel,
        in_specs=[pl.BlockSpec(memory_space=pltpu.SMEM)] + [vmem] * 6,
        out_specs=pl.BlockSpec(memory_space=pl.ANY),
        out_shape=jax.ShapeDtypeStruct((peers, lines, PACK), bf16),
        scratch_shapes=[
            pltpu.VMEM((hidden // PACK, peers, up_rows, PACK), bf16),
            pltpu.VMEM((width // PACK, peers, down_rows, PACK), bf16),
            pltpu.SemaphoreType.DMA((2, hidden // PACK)),
            pltpu.SemaphoreType.DMA((2, width // PACK // 2)),
        ],
        compiler_params=pltpu.CompilerParams(vmem_limit_bytes=56 * 2**20),
        cost_estimate=pl.CostEstimate(
            flops=4 * width * inputs[0].shape[0] * hidden, bytes_accessed=4 * width * hidden, transcendentals=0
        ),
        name="mlp_grads",
    )(core, *inputs, grad_hidden, activated, *grads)


def tail_kernel(core_ref, x_ref, g_ref, w_ref, n_ref, small_ref, lines_ref, keep_ref, give_ref):
    cols, some = g_ref.shape[1], x_ref.shape[0] // 2
    ones = jnp.ones((x_ref.shape[0], 128), bf16)
    part = mm_nt(g_ref[...], w_ref[...])
    low = part.astype(bf16)
    first = mm_tn(low, ones)
    second = mm_tn((part * n_ref[...].astype(f32)).astype(bf16), ones)
    lane = lax.broadcasted_iota(jnp.int32, first.shape, 1)
    small = jnp.where(lane == 6, first, jnp.where(lane == 7, second, small_ref[...]))
    lines_ref[:, cols:] = small.astype(bf16)
    zero = core_ref[0] == 0
    keep_ref[...] = jnp.where(zero, low[:some], low[some:])
    give_ref[...] = jnp.where(zero, low[some:], low[:some])
    half = x_ref.shape[1] // 2
    for k in range(2):
        rows = pl.ds(k * half, half)
        lines_ref[rows, :cols] = mm_tn(x_ref[:, rows], g_ref[...]).astype(bf16)


def tail(core, inputs, grad, weight, norm, small):
    rows, width = inputs.shape
    out = [
        jax.ShapeDtypeStruct((width, grad.shape[1] + 128), bf16),
        jax.ShapeDtypeStruct((rows // 2, width), bf16),
        jax.ShapeDtypeStruct((rows // 2, width), bf16),
    ]
    vmem = pl.BlockSpec(memory_space=pltpu.VMEM)
    return pl.pallas_call(
        tail_kernel,
        in_specs=[pl.BlockSpec(memory_space=pltpu.SMEM)] + [vmem] * 5,
        out_specs=[vmem] * 3,
        out_shape=out,
        compiler_params=pltpu.CompilerParams(vmem_limit_bytes=56 * 2**20),
        cost_estimate=pl.CostEstimate(flops=8 * 10**9, bytes_accessed=10**7, transcendentals=0),
        name="tail",
    )(core, inputs, grad, weight, norm, small)


def inverse_freq(pair_total):
    return 1.0 / 10000.0 ** (jnp.arange(pair_total, dtype=f32) * 2.0 / (2.0 * pair_total))


def rotary_tables(places):
    pair_count = HEAD_DIM // 2
    side = pair_count // 3
    frame = pair_count - 2 * side
    freq = jnp.concatenate([inverse_freq(frame), inverse_freq(side), inverse_freq(side)])
    freq = jnp.repeat(freq, 2)[None, :]
    pair = lax.broadcasted_iota(jnp.int32, (1, HEAD_DIM), 1) // 2
    angles = jnp.where(
        pair < frame,
        places[0][:, None],
        jnp.where(pair < frame + side, places[1][:, None], places[2][:, None]),
    ) * freq
    return jnp.cos(angles), jnp.sin(angles)


def columns_for(weight, count, owners):
    rows = weight.shape[0]
    parts = jnp.transpose(weight.reshape(rows, count, owners, -1), (2, 0, 1, 3))
    return parts.reshape(owners, rows, -1)


def along_line(parts):
    return lax.all_to_all(parts, LINE, split_axis=0, concat_axis=0, tiled=True)


def for_line(group_parts=None, core_parts=None):
    if core_parts is not None:
        group_parts = jnp.repeat(core_parts, 2, axis=0)
    return jnp.concatenate([group_parts, group_parts], 0)


def first_then(first, *then):
    return lax.optimization_barrier((first, *then))[1:]


def on_device(
    latent_tokens, time_embed, text_tokens, positions,
    w_qkv, attn_out, cross_q, cross_kv, cross_out, mlp_in, mlp_out,
    gain_q, gain_k, gain_cq, gain_ck, norm_weight, norm_bias, modulation, cotangent,
):
    peers = lax.axis_size(PLACES)
    core, zl = lax.axis_index("core"), lax.axis_index("zl")
    width = latent_tokens.shape[2]
    half, local = width // 2, width // 4
    clips = 2
    rows_each = w_qkv.shape[0]
    line_rows = 8 * rows_each
    hid_each = mlp_out.shape[0]
    hid_pad = -(-hid_each * peers // 256) * 256 // peers
    hidden = peers * hid_pad

    x_mine = latent_tokens[0]
    x_wide = join(join(x_mine, "zl", 0), "core", 0)
    text = join(join(text_tokens[0], "zl", 0), "core", 0)
    small = jnp.concatenate(
        [v[None] for v in (gain_q, gain_k, gain_cq, gain_ck, norm_weight, norm_bias)] + [modulation], 0
    )
    small = jnp.pad(small.T, ((0, 0), (0, 116)))
    shard = along_line(
        jnp.concatenate(
            [
                for_line(group_parts=columns_for(w_qkv, 3, 4)),
                for_line(core_parts=columns_for(attn_out, 1, 2)),
                jnp.broadcast_to(small, (8, *small.shape)),
            ],
            axis=2,
        )
    ).reshape(line_rows, -1)
    first_weight = lax.all_gather(shard[:, : 3 * local + half], PLACES, axis=0, tiled=True)
    qkv_weight, out_weight = first_weight[:, : 3 * local], first_weight[:, 3 * local :]
    whole = shard[:, 3 * local + half : 3 * local + half + 12].T.reshape(1, -1)
    whole = axis_join(axis_join(whole, "x"), "y").reshape(peers, 12, line_rows)
    whole = jnp.transpose(whole, (1, 0, 2)).reshape(12, width).astype(f32)

    parts = jnp.concatenate(
        [columns_for(cross_q, 1, 2), columns_for(cross_kv, 2, 2), columns_for(cross_out, 1, 2)], axis=2
    )
    whole, parts = lax.optimization_barrier((whole, parts))
    cross_shard = along_line(for_line(core_parts=parts)).reshape(line_rows, -1)
    cross_weight = lax.all_gather(cross_shard, PLACES, axis=0, tiled=True)
    cq_weight = cross_weight[:, :half]
    ckv_weight = cross_weight[:, half : 3 * half]
    co_weight = cross_weight[:, 3 * half :]

    time_rows = join(time_embed, "core", 0)
    mod_wide = time_rows + whole[None, 6:]
    mod_mine = time_embed[0] + whole[6:]

    def here(rows, cut):
        picked = jnp.split(rows, 2, -1)
        rows = jnp.where(core == 0, picked[0], picked[1])
        if cut == 4:
            picked = jnp.split(rows, 2, -1)
            rows = jnp.where(zl == 0, picked[0], picked[1])
        return rows

    mod = here(mod_wide, 2)
    g_q, g_k = here(whole[0:1], 4), here(whole[1:2], 4)
    g_cq, g_ck, n_w, n_b = (here(whole[i : i + 1], 2) for i in range(2, 6))
    tokens = latent_tokens.shape[1]

    def per_clip(row):
        rows = mod[:, row]
        return jnp.broadcast_to(rows[:, None], (clips, tokens, half)).reshape(-1, half)

    places = join(join(positions[0].astype(f32), "zl", 1), "core", 1)
    cos, sin = rotary_tables(places)
    x_here = trade(x_mine, "core", 1, 0).astype(f32)
    up_here = trade(cotangent[0], "core", 1, 0).astype(f32)
    norm_wide, _ = layer_norm(x_wide.astype(f32))
    attn_input = norm_wide.reshape(clips, -1, width) * (1.0 + mod_wide[:, 1:2]) + mod_wide[:, 0:1]
    attn_input = flat(attn_input).astype(bf16)
    attn_input, text, x_here, up_here = lax.optimization_barrier((attn_input, text, x_here, up_here))

    qkv = mm(attn_input, qkv_weight)
    squares = jnp.sum((qkv * qkv).reshape(-1, 3, local)[:, :2], axis=-1).T
    inv_qk = lax.rsqrt(group_sum(squares) / width + NORM_EPS).T
    qr, kr, vb, heads = self_forward(qkv, inv_qk, g_q, g_k, cos, sin, clips)
    heads = flat(trade(heads.reshape(2, -1, local), "zl", 1, 2))
    attn_tokens = join(heads, "core", 1)

    up = mlp_in.reshape(rows_each, peers, 8, hid_each)
    up = jnp.pad(up, ((0, 0), (0, 0), (0, 0), (0, hid_pad - hid_each)))
    up = jnp.transpose(up, (2, 0, 1, 3)).reshape(8, rows_each, hidden)
    attn_tokens, up = lax.optimization_barrier((attn_tokens, up))
    up_shard = along_line(up).reshape(line_rows, hidden)
    down = jnp.pad(mlp_out, ((0, hid_pad - hid_each), (0, 0)))
    mlp_shard = jnp.concatenate(
        [up_shard[:, at : at + PACK] for at in range(0, hidden, PACK)]
        + [down[:, at : at + PACK] for at in range(0, width, PACK)],
        axis=0,
    )
    mlp_pack = lax.all_gather(mlp_shard, PLACES, axis=0)

    branch_one = mm(attn_tokens, out_weight)
    after_attn = x_here + branch_one * per_clip(2)
    norm_two, inv_two = split_norm(after_attn)
    cross_input = join((norm_two * n_w + n_b).astype(bf16), "core", 1)
    grad_three = (up_here * per_clip(5)).astype(bf16)
    cross_input, grad_three = lax.optimization_barrier((cross_input, grad_three))
    grad_three = others(grad_three, CHIPS)

    ckv = mm(text, ckv_weight)
    ck_pre = ckv[:, :half]
    inv_ck = lax.rsqrt(core_sum(jnp.sum(ck_pre * ck_pre, axis=-1)[None]) / width + NORM_EPS)[0]
    cross_key = (ck_pre * inv_ck[:, None] * g_ck).astype(bf16)
    cross_value = ckv[:, half:].astype(bf16)
    cq_pre = mm(cross_input, cq_weight)
    cq_pre, *grad_three = lax.optimization_barrier((cq_pre, *grad_three))

    def both_cores(pieces):
        lines = jnp.concatenate(pieces, 0)
        return lines, swap(lines, "core")

    grad_three = both_cores(grad_three)
    inv_cq = lax.rsqrt(core_sum(jnp.sum(cq_pre * cq_pre, axis=-1)[None]) / width + NORM_EPS)[0]
    cross_query, cross_heads = cross_forward(cq_pre, inv_cq[:, None], g_cq, cross_key, cross_value)
    cross_tokens = join(cross_heads, "core", 1)
    after_cross = after_attn + mm(cross_tokens, co_weight)

    norm_three, inv_three = split_norm(after_cross)
    mlp_input = (norm_three * (1.0 + per_clip(4)) + per_clip(3)).astype(bf16)
    mlp_input = both_cores(others(mlp_input, CHIPS))
    core_row = jnp.full((1,), core, jnp.int32)
    activated, grad_hidden, keep, give = mlp(
        core_row, mlp_input, grad_three, mlp_pack, line_rows, hidden, hid_pad
    )

    def core_lines(keep, give):
        lines = keep.astype(f32) + swap(give, "core").astype(f32)
        return lines[: 2 * tokens], jnp.split(lines[2 * tokens :].astype(bf16), 3, 0)

    near, far = core_lines(keep, give)
    grad_mlp_input = near_sum([near, *far], CHIPS)
    down_weight = jnp.concatenate(
        [
            mlp_pack[:, at : at + hid_pad].reshape(hidden, PACK)
            for at in range(line_rows * (hidden // PACK), mlp_pack.shape[1], hid_pad)
        ],
        axis=1,
    )
    near, far = core_lines(*halves(mm(activated, down_weight).astype(bf16), "core", 1))
    mlp_lines = mlp_grads(core_row, mlp_input, grad_hidden, activated, grad_three, peers)
    mlp_lines = mlp_lines.reshape(-1, PACK)
    mlp_sum = lax.psum_scatter(mlp_lines, PLACES, scatter_dimension=0, tiled=True)

    def norm_back(grad, scaled, norm, inv):
        sums = core_sum(jnp.stack([jnp.sum(scaled, axis=-1), jnp.sum(scaled * norm, axis=-1)])) / width
        return (scaled - sums[0][:, None] - norm * sums[1][:, None]) * inv[:, None]

    grad_mod3 = jnp.sum(grad_mlp_input, axis=0)
    grad_mod4 = jnp.sum(grad_mlp_input * norm_three, axis=0)
    grad_cross = up_here + norm_back(
        grad_mlp_input, grad_mlp_input * (1.0 + per_clip(4)), norm_three, inv_three
    )
    grad_two = grad_cross.astype(bf16)

    grad_heads = scatter_sum(mm_nt(grad_two, co_weight).astype(bf16), "core", 1).astype(bf16)
    rest_lines = tn_pack(cross_tokens, grad_two, 4, 5, peers)
    grad_heads, near, *far = lax.optimization_barrier((grad_heads, near, *far))
    far = [lax.ppermute(far[k], CHIPS, [(i, i ^ (k + 1)) for i in range(4)]) for k in range(3)]
    up_cq, up_ck, up_cv = cross_backward(cross_query, cross_key, cross_value, grad_heads)
    up_cq, *far = lax.optimization_barrier((up_cq, *far))
    branch_three = near + sum(part.astype(f32) for part in far)
    result_here = (after_cross + branch_three * per_clip(5)).astype(bf16)
    grad_mod5 = jnp.sum(up_here * branch_three, axis=0)
    result = trade(result_here, "core", 0, 1)

    def rms_back(grad, pre, inv, gain):
        mean = core_sum(jnp.sum(grad * pre * gain, axis=-1)[None])[0] / width
        gain_grad = jnp.sum(grad * pre * inv[:, None], axis=0)
        return (grad * gain - pre * (inv * inv * mean)[:, None]) * inv[:, None], gain_grad

    grad_cq, grad_gain_cq = rms_back(up_cq, cq_pre, inv_cq, g_cq)
    grad_cq = grad_cq.astype(bf16)
    grad_cross_input = scatter_sum(mm_nt(grad_cq, cq_weight).astype(bf16), "core", 1)
    grad_ck, grad_gain_ck = rms_back(up_ck, ck_pre, inv_ck, g_ck)
    grad_ckv = jnp.concatenate([grad_ck.astype(bf16), up_cv], axis=1)
    rest_lines = tn_pack(cross_input, grad_cq, 1, 5, peers, rest_lines)
    rest_lines = tn_pack(text, grad_ckv, 2, 5, peers, rest_lines)
    grad_n_w = jnp.sum(grad_cross_input * norm_two, axis=0)
    grad_n_b = jnp.sum(grad_cross_input, axis=0)
    grad_attn = grad_cross + norm_back(grad_cross_input, grad_cross_input * n_w, norm_two, inv_two)
    grad_attn_mine = trade(grad_attn, "core", 0, 1)

    grad_one = (grad_attn * per_clip(2)).astype(bf16)
    grad_mod2 = jnp.sum(grad_attn * branch_one, axis=0)
    grad_heads = scatter_sum(mm_nt(grad_one, out_weight).astype(bf16), "core", 1).astype(bf16)
    grad_heads = flat(trade(by_seq(grad_heads), "zl", 2, 1))
    rest_lines = tn_pack(attn_tokens, grad_one, 0, 5, peers, rest_lines)
    mlp_sum, rest_lines = lax.optimization_barrier((mlp_sum, rest_lines))
    rest_sum = lax.psum_scatter(rest_lines.reshape(-1, REST), PLACES, scatter_dimension=0, tiled=True)
    up_q, up_k, grad_v, part, dgain = self_backward(
        qr, kr, vb, grad_heads, qkv, inv_qk, g_q, g_k, cos, sin, clips
    )
    mean_qk = group_sum(part.T) / width
    pull = (mean_qk * (inv_qk * inv_qk).T).T
    grad_q = (up_q - qkv[:, :local] * pull[:, 0:1]) * inv_qk[:, 0:1]
    grad_k = (up_k - qkv[:, local : 2 * local] * pull[:, 1:2]) * inv_qk[:, 1:2]
    grad_qkv = jnp.concatenate([grad_q.astype(bf16), grad_k.astype(bf16), grad_v], axis=1)
    dgain = jnp.transpose(jnp.sum(dgain, axis=0), (1, 0, 2)).reshape(2, local)

    dgain = jnp.where(zl == 0, jnp.pad(dgain, ((0, 0), (0, local))), jnp.pad(dgain, ((0, 0), (local, 0))))
    halfs = jnp.concatenate(
        [
            dgain,
            jnp.stack(
                [
                    grad_gain_cq, grad_gain_ck, grad_n_w, grad_n_b,
                    jnp.zeros_like(grad_n_b), jnp.zeros_like(grad_n_b),
                    grad_mod2, grad_mod3, grad_mod4, grad_mod5,
                ]
            ),
        ],
        0,
    )
    smalls = jnp.where(
        core == 0, jnp.pad(halfs, ((0, 0), (0, half))), jnp.pad(halfs, ((0, 0), (half, 0)))
    )
    small_cols = jnp.pad(smalls.T, ((0, 0), (0, 116)))
    last_lines, keep, give = tail(
        core_row, attn_input, grad_qkv, qkv_weight, norm_wide.astype(bf16), small_cols
    )
    last_parts = lax.all_to_all(
        last_lines.reshape(peers, line_rows, -1), PLACES, split_axis=0, concat_axis=0, tiled=True
    )

    grad_attn_input = keep.astype(f32) + swap(give, "core").astype(f32)
    grad_attn_input = scatter_sum(grad_attn_input, "zl", 0)
    norm_one, inv_one = layer_norm(x_mine.astype(f32))
    scaled = grad_attn_input * (1.0 + mod_mine[1:2])
    input_grad = grad_attn_mine + inv_one * (
        scaled
        - jnp.mean(scaled, axis=-1, keepdims=True)
        - norm_one * jnp.mean(scaled * norm_one, axis=-1, keepdims=True)
    )
    mlp_sum, input_grad, last_parts, rest_sum = lax.optimization_barrier(
        (mlp_sum, input_grad, last_parts, rest_sum)
    )
    up_lines = line_rows * (hidden // PACK)
    last_sum = jnp.sum(last_parts.astype(f32), axis=0).astype(bf16)
    rest = jnp.concatenate(
        jnp.split(rest_sum, 5, 0) + [last_sum] + jnp.split(mlp_sum[:up_lines], hidden // PACK, 0), axis=1
    )
    lines = along_line(rest.reshape(8, rows_each, -1))
    up_rows = lines[..., -hidden:].reshape(8, rows_each, peers, hid_pad)[..., :hid_each]
    grad_mlp_in = jnp.transpose(up_rows, (1, 2, 0, 3)).reshape(rows_each, -1).astype(f32)
    down_rows = jnp.concatenate(jnp.split(mlp_sum[up_lines:], width // PACK, 0), axis=1)
    grad_mlp_out = down_rows[:hid_each].astype(f32)
    lines = lines[..., :-hidden].astype(f32).reshape(2, 2, 2, rows_each, -1)
    sides = lines[0, :, 0] + lines[0, :, 1] + lines[1, :, 0] + lines[1, :, 1]
    qkv_lines = (lines[0] + lines[1]).reshape(4, rows_each, -1)[..., 5 * REST : 5 * REST + 3 * local]
    grad_qkv_rows = jnp.transpose(qkv_lines.reshape(4, rows_each, 3, local), (1, 2, 0, 3))
    grad_qkv_rows = grad_qkv_rows.reshape(rows_each, -1)
    small_sum = (sides[0] + sides[1])[:, 5 * REST + 3 * local : 5 * REST + 3 * local + 12].T

    def whole_of(first, count):
        return jnp.concatenate(
            [
                sides[side, :, at * REST : (at + 1) * REST]
                for at in range(first, first + count)
                for side in range(2)
            ],
            axis=1,
        )

    return (
        result[None],
        input_grad[None],
        grad_qkv_rows, whole_of(0, 1), whole_of(1, 1), whole_of(2, 2), whole_of(4, 1),
        grad_mlp_in, grad_mlp_out,
        small_sum[0], small_sum[1], small_sum[2], small_sum[3], small_sum[4], small_sum[5],
        small_sum[6:],
    )


def solution(mesh):
    places = mesh.devices.size // 8
    across = min(places, 4)
    lines = Mesh(
        mesh.devices.reshape(places // across, across, 2, 2, 2), ("y", "x", "zh", "core", "zl")
    )
    clip = ("y", "x", "zh", "core")
    every = (*clip, "zl")
    tokens = P(clip, "zl", None)
    rows = P(every, None)
    return jax.shard_map(
        on_device,
        mesh=lines,
        in_specs=(tokens, P(clip, None, None), tokens, P(clip, None, "zl"))
        + (rows,) * 7 + (P(every),) * 6 + (P(None, every), tokens),
        out_specs=(tokens, tokens) + (rows,) * 7 + (P(every),) * 6 + (P(None, every),),
        check_vma=False,
    )
```

time: 2690 us -> 570 us (0.21)
  waiting for transfers between devices: 1470 us -> 203 us
  local copies, waits for them, and re-layouts: 813 us -> 47.6 us
  matrix products: 208 us -> 33.9 us
  Pallas kernels: 0 us -> 100 us
  other arithmetic: 119 us -> 56.2 us
  starting transfers between devices: 9.72 us -> 60.3 us
    unnamed x10 -> x5, waiting for transfers between devices: 743 us -> 0.08 us
    all_gather x4 -> x3, waiting for transfers between devices: 731 us -> 0.01 us  [the longest x1 0.01 us: on_device(): lax.all_gather(shard[:, :3 * local + half], PLACES, axis=0, tiled=True)]
    another operation x25 -> x9, local copies, waits for them, and re-layouts: 281 us -> 0.84 us  [the longest x1 0.81 us: on_device(): inv_cq[:, None]]
    reshape x30 -> x21, local copies, waits for them, and re-layouts: 217 us -> 7.99 us  [the longest x7 1.99 us: columns_for(): parts = jnp.transpose(weight.reshape(rows, count, owners, -1), (2, 0, 1, 3))]
    dot_general x32 -> x9, matrix products: 208 us -> 33.9 us  [the longest x6 26 us: mm(): return jnp.dot(left, right, preferred_element_type=f32)]
    ppermute x0 -> x57, waiting for transfers between devices: none -> 124 us  [the longest x37 57.1 us: swap(): return lax.ppermute(array, axis_name, SWAP)]
    unnamed x303 -> x149, local copies, waits for them, and re-layouts: 138 us -> 16.6 us
    pallas_call x0 -> x11, Pallas kernels: none -> 100 us  [the longest x4 20.2 us: tn_pack(): pl.pallas_call(functools.partial(tn_pack_kernel, place), in_specs=[vmem,...]
  transfers between devices with their start and end apart: 10 -> 64, of which waited for: 4 -> 34; matrix products, arithmetic and copies ran while one was open for 22% -> 19% of each run, Pallas kernels for 0% -> 12%
where the time goes in v1:
time: 570 us; the launch traced here: 562 us
  waiting for transfers between devices  203 us (36%)
  Pallas kernels  100 us (18%)
  starting transfers between devices  60.3 us (11%)
  other arithmetic  56.2 us (10%)
  local copies, waits for them, and re-layouts  47.6 us (8%)
  blocking collectives  44.4 us (8%)
  matrix products  33.9 us (6%)
  between operations  16.1 us (3%)
    ppermute x37, waiting for transfers between devices, swap(): return lax.ppermute(array, axis_name, SWAP)  57.1 us
    all_to_all x1, waiting for transfers between devices, on_device(): lax.all_to_all(last_lines.reshape(peers, line_rows, -1), PLACES, split_ax...  54.4 us
    all_to_all x3, blocking collectives, along_line(): return lax.all_to_all(parts, LINE, split_axis=0, concat_axis=0, tiled=True)  44.4 us
    ppermute x12, waiting for transfers between devices, others(): lax.ppermute(array, axis_name, [(i, i ^ k) for i in range(size)])  35.7 us
    ppermute x37, starting transfers between devices, swap(): return lax.ppermute(array, axis_name, SWAP)  26.4 us
    dot_general x6, matrix products, mm(): return jnp.dot(left, right, preferred_element_type=f32)  26 us
    all_to_all x1, waiting for transfers between devices, along_line(): return lax.all_to_all(parts, LINE, split_axis=0, concat_axis=0, tiled=True)  20.6 us
    pallas_call x4, Pallas kernels, tn_pack(): pl.pallas_call(functools.partial(tn_pack_kernel, place), in_specs=[vmem,...  20.2 us
  transfers between devices with their start and end apart: 64, of which 34 were waited for; matrix products, arithmetic and copies ran while one was open for 19% of the time, Pallas kernels for 12%

profile of v1, /device:TPU:1, one launch (start us, length us, event | category | flops | bytes accessed | tf_op | source)
XLA Modules:
  0.0 562.1 jit_solution(9566853502355503974)
XLA Ops:
  11.4 15.8 %all_to_all.25 = bf16[8,12,2048]{2,1,0:T(8,128)(2,1)S(1)} all-to-all(bf16[8,12,2048]{2,1,0:T(8,128)(2,1)S(1)} %copy.186), channel_id=1, replica_groups=mesh['y'=4,'x'=4,'zh'=2,'core'=2,'zl'=2] {'zh','core','zl'}, dimensions={0} | all-to-all | bytes 786432 | tf_op jit(solution)/shard_map/all_to_all | solution.py:568
  42.3 18.6 %all_to_all.26 = bf16[8,12,3072]{2,1,0:T(8,128)(2,1)S(1)} all-to-all(bf16[8,12,3072]{2,1,0:T(8,128)(2,1)S(1)} %pad_maximum_fusion.3), channel_id=1, replica_groups=mesh['y'=4,'x'=4,'zh'=2,'core'=2,'zl'=2] {'zh','core','zl'}, dimensions={0} | all-to-all | bytes 1179648 | tf_op jit(solution)/shard_map/all_to_all | solution.py:568
  65.5 8.5 %collective-permute-done.16 = f32[3,128]{1,0:T(4,128)S(1)} collective-permute-done((f32[3,128]{1,0:T(4,128)S(1)}, f32[3,128]{1,0:T(4,128)S(1)}, u32[]{:S(2)}, u32[]{:S(2)}) %collective-permute-start.16) | collective-permute-done | bytes 1568 | tf_op jit(solution)/shard_map/ppermute | solution.py:40
  80.1 14.3 %collective-permute-done.9 = bf16[256,1536]{1,0:T(8,128)(2,1)S(1)} collective-permute-done((bf16[256,1536]{1,0:T(8,128)(2,1)S(1)}, bf16[256,1536]{1,0:T(8,128)(2,1)S(1)}, u32[]{:S(2)}, u32[]{:S(2)}) %collective-permute-start.9) | collective-permute-done | bytes 786464 | tf_op jit(solution)/shard_map/ppermute | solution.py:40
  104.5 6.5 %fusion.92 = (f32[512,1152]{1,0:T(8,128)}, f32[512,1152]{1,0:T(8,128)}) fusion(bf16[512,1536]{1,0:T(8,128)(2,1)S(1)} %get-tuple-element.69.x_ref, bf16[1536,1920]{1,0:T(8,128)(2,1)} %all-gather.5.cloned.1.call-done), kind=kOutput, calls=%fused_computation.334 | convolution fusion | flops 1812529152 | bytes 9830400 | tf_op jit(solution)/shard_map/dot_general | solution.py:28
  115.9 5.5 collective-permute-done.13
  121.4 6.1 %collective-permute-done.15 = f32[2,512]{0,1:T(8,128)S(1)} collective-permute-done((f32[2,512]{0,1:T(8,128)S(1)}, f32[2,512]{0,1:T(8,128)S(1)}, u32[]{:S(2)}, u32[]{:S(2)}) %collective-permute-start.15) | collective-permute-done | bytes 4128 | tf_op jit(solution)/shard_map/ppermute | solution.py:78
  128.2 7.4 %self_forward.1 = (bf16[512,384]{1,0:T(8,128)(2,1)}, bf16[512,384]{1,0:T(8,128)(2,1)}, bf16[512,384]{1,0:T(8,128)(2,1)}, bf16[512,384]{1,0:T(8,128)(2,1)}) custom-call(f32[512,1152]{1,0:T(8,128)} %get-tuple-element.351.q_ref.k_ref.v_ref, f32[512,1152]{1,0:T(8,128)} %get-tuple-element.351.q_ref.k_ref.v_ref, f32[512,1152]{1,0:T(8,128)} %get-tuple-element.351.q_ref.k_ref.v_ref, ...), custom_call_target="tpu_custom_call" | custom-call | flops 8000000000 | bytes 10000000 | tf_op jit(solution)/shard_map/self_forward/pallas_call | solution.py:191
  137.0 6.4 %collective-permute-done.18 = bf16[2,128,384]{2,1,0:T(8,128)(2,1)S(1)} collective-permute-done((bf16[2,128,384]{2,1,0:T(8,128)(2,1)S(1)}, bf16[2,128,384]{2,1,0:T(8,128)(2,1)S(1)}, u32[]{:S(2)}, u32[]{:S(2)}) %collective-permute-start.18) | collective-permute-done | bytes 196640 | tf_op jit(solution)/shard_map/ppermute | solution.py:40
  146.4 10.0 %all_to_all.27 = bf16[8,12,1280]{2,1,0:T(8,128)(2,1)S(1)} all-to-all(bf16[8,12,1280]{2,1,0:T(8,128)(2,1)S(1)} %copy.195), channel_id=1, replica_groups=mesh['y'=4,'x'=4,'zh'=2,'core'=2,'zl'=2] {'zh','core','zl'}, dimensions={0} | all-to-all | bytes 491520 | tf_op jit(solution)/shard_map/all_to_all | solution.py:568
  175.7 9.1 %collective-permute-done.23 = bf16[256,768]{1,0:T(8,128)(2,1)} collective-permute-done((bf16[256,768]{1,0:T(8,128)(2,1)S(1)}, bf16[256,768]{1,0:T(8,128)(2,1)}, u32[]{:S(2)}, u32[]{:S(2)}) %collective-permute-start.23) | collective-permute-done | bytes 393248 | tf_op jit(solution)/shard_map/ppermute | solution.py:46
  189.0 6.9 %fusion = f32[1024,1536]{1,0:T(8,128)S(1)} fusion(bf16[1024,1536]{1,0:T(8,128)(2,1)S(1)} %copy-done.3, bf16[1536,3072]{1,0:T(8,128)(2,1)} %all-gather.7.cloned.1.call-done), kind=kOutput, calls=%fused_computation | convolution fusion | flops 4831838208 | bytes 14155776 | tf_op jit(solution)/shard_map/dot_general | solution.py:28
  200.1 4.1 multiply_convert_fusion.1.k_ref
  204.2 7.9 %cross_forward.1 = (bf16[256,768]{1,0:T(8,128)(2,1)}, bf16[256,768]{1,0:T(8,128)(2,1)}) custom-call(f32[256,768]{1,0:T(8,128)} %copy-done.8, f32[256,1]{1,0:T(8,128)} %copy.194.r_ref, f32[1,768]{1,0:T(1,128)} %get-tuple-element.262.g_ref, bf16[1024,768]{1,0:T(8,128)(2,1)} %multiply_convert_fusion.1.k_ref, bf16[1024,768]{1,0:T(8,128)(2,1)} %slice.605.v_ref), custom_call_target="tpu_custom_call" | custom-call | flops 8999999488 | bytes 10000000 | tf_op jit(solution)/shard_map/cross_forward/pallas_call | solution.py:272
  230.7 9.2 %collective-permute-done.30 = bf16[256,768]{1,0:T(8,128)(2,1)S(1)} collective-permute-done((bf16[256,768]{1,0:T(8,128)(2,1)S(1)}, bf16[256,768]{1,0:T(8,128)(2,1)S(1)}, u32[]{:S(2)}, u32[]{:S(2)}) %collective-permute-start.30) | collective-permute-done | bytes 393248 | tf_op jit(solution)/shard_map/ppermute | solution.py:46
  248.1 19.2 %mlp.1 = (bf16[1024,1280]{1,0:T(8,128)(2,1)}, bf16[1024,1280]{1,0:T(8,128)(2,1)}, bf16[1024,768]{1,0:T(8,128)(2,1)}, bf16[1024,768]{1,0:T(8,128)(2,1)}) custom-call(s32[1]{0:T(128)} %bitcast.47.core_ref, bf16[1024,768]{1,0:T(8,128)(2,1)} %copy-done.23, bf16[1024,768]{1,0:T(8,128)(2,1)} %collective-permute-done.32.xo_ref, bf16[1024,768]{1,0:T(8,128)(2,1)} %copy-done.47, ...), custom_call_target="tpu_custom_call" | custom-call | flops 12079595520 | bytes 7864320 | tf_op jit(solution)/shard_map/mlp/pallas_call | solution.py:383
  267.4 14.7 %mlp_grads.1 = bf16[16,960,256]{2,1,0:T(8,128)(2,1)} custom-call(s32[1]{0:T(128)} %bitcast.47.core_ref, bf16[1024,768]{1,0:T(8,128)(2,1)} %copy-done.23, bf16[1024,768]{1,0:T(8,128)(2,1)} %collective-permute-done.32.xo_ref, bf16[1024,1280]{1,0:T(8,128)(2,1)} %get-tuple-element.97.gh_ref, bf16[1024,1280]{1,0:T(8,128)(2,1)} %get-tuple-element.86.act_ref, ...), custom_call_target="tpu_custom_call" | custom-call | flops 8053063680 | bytes 7864320 | tf_op jit(solution)/shard_map/mlp_grads/pallas_call | solution.py:485
  286.9 4.4 convolution_convert_fusion
  297.2 6.7 %collective-permute-done.35 = bf16[256,768]{1,0:T(8,128)(2,1)S(1)} collective-permute-done((bf16[256,768]{1,0:T(8,128)(2,1)S(1)}, bf16[256,768]{1,0:T(8,128)(2,1)S(1)}, u32[]{:S(2)}, u32[]{:S(2)}) %collective-permute-start.35) | collective-permute-done | bytes 393248 | tf_op jit(solution)/shard_map/ppermute | solution.py:72
  303.9 9.8 %collective-permute-done.36 = bf16[256,768]{1,0:T(8,128)(2,1)S(1)} collective-permute-done((bf16[256,768]{1,0:T(8,128)(2,1)S(1)}, bf16[256,768]{1,0:T(8,128)(2,1)S(1)}, u32[]{:S(2)}, u32[]{:S(2)}) %collective-permute-start.36) | collective-permute-done | bytes 393248 | tf_op jit(solution)/shard_map/ppermute | solution.py:72
  330.7 9.8 %cross_backward.1 = (f32[256,768]{1,0:T(8,128)}, f32[1024,768]{1,0:T(8,128)}, bf16[1024,768]{1,0:T(8,128)(2,1)}) custom-call(bf16[256,768]{1,0:T(8,128)(2,1)} %get-tuple-element.88.qn_ref, bf16[1024,768]{1,0:T(8,128)(2,1)} %multiply_convert_fusion.1.k_ref, bf16[1024,768]{1,0:T(8,128)(2,1)} %slice.605.v_ref, bf16[256,768]{1,0:T(8,128)(2,1)} %add_convert_fusion.1.do_ref), custom_call_target="tpu_custom_call" | custom-call | flops 11000000512 | bytes 10000000 | tf_op jit(solution)/shard_map/cross_backward/pallas_call | solution.py:300
  366.6 9.4 %tn_pack.6.rest_0_ = bf16[16,480,768]{2,1,0:T(8,128)(2,1)} custom-call(bf16[1024,1536]{1,0:T(8,128)(2,1)} %maximum_select_fusion.x_ref, bf16[1024,1536]{1,0:T(8,128)(2,1)} %pad_maximum_fusion.g_ref, bf16[16,480,768]{2,1,0:T(8,128)(2,1)} %tn_pack.5.rest_0_), custom_call_target="tpu_custom_call", output_to_operand_aliasing={{}: (2, {})} | custom-call | flops 4831838208 | bytes 4718592 | tf_op jit(solution)/shard_map/tn_pack/pallas_call | solution.py:436
  387.6 4.6 slice.394.w_ref
  394.9 10.3 %self_backward.1 = (f32[512,384]{1,0:T(8,128)}, f32[512,384]{1,0:T(8,128)}, bf16[512,384]{1,0:T(8,128)(2,1)}, f32[512,2]{1,0:T(8,128)}, f32[2,3,2,128]{3,2,1,0:T(2,128)}) custom-call(bf16[512,384]{1,0:T(8,128)(2,1)} %get-tuple-element.102.qr_ref, bf16[512,384]{1,0:T(8,128)(2,1)} %get-tuple-element.103.kr_ref, bf16[512,384]{1,0:T(8,128)(2,1)} %get-tuple-element.104.vb_ref, ...), custom_call_target="tpu_custom_call" | custom-call | flops 11000000512 | bytes 10000000 | tf_op jit(solution)/shard_map/self_backward/pallas_call | solution.py:241
  412.9 6.7 %collective-permute-done.54 = f32[2,512]{0,1:T(8,128)} collective-permute-done((f32[2,512]{0,1:T(8,128)}, f32[2,512]{0,1:T(8,128)}, u32[]{:S(2)}, u32[]{:S(2)}) %collective-permute-start.54) | collective-permute-done | bytes 4128 | tf_op jit(solution)/shard_map/ppermute | solution.py:78
  422.9 10.7 %tail.1 = (bf16[1536,1280]{1,0:T(8,128)(2,1)}, bf16[256,1536]{1,0:T(8,128)(2,1)}, bf16[256,1536]{1,0:T(8,128)(2,1)}) custom-call(s32[1]{0:T(128)} %bitcast.47.core_ref, bf16[512,1536]{1,0:T(8,128)(2,1)} %copy-done.24, bf16[512,1152]{1,0:T(8,128)(2,1)} %pad_maximum_fusion.2.g_ref, bf16[1536,1152]{1,0:T(8,128)(2,1)} %slice.394.w_ref, ...), custom_call_target="tpu_custom_call" | custom-call | flops 8000000000 | bytes 10000000 | tf_op jit(solution)/shard_map/tail/pallas_call | solution.py:531
  433.7 5.0 all-to-all-start.3
  443.7 8.2 %collective-permute-done.56 = bf16[128,1536]{1,0:T(8,128)(2,1)S(1)} collective-permute-done((bf16[128,1536]{1,0:T(8,128)(2,1)S(1)}, bf16[128,1536]{1,0:T(8,128)(2,1)S(1)}, u32[]{:S(2)}, u32[]{:S(2)}) %collective-permute-start.56) | collective-permute-done | bytes 393248 | tf_op jit(solution)/shard_map/ppermute | solution.py:40
  453.5 54.4 %all-to-all-done.3 = bf16[16,96,1280]{2,1,0:T(8,128)(2,1)} async-done(((bf16[16,96,1280]{2,1,0:T(8,128)(2,1)}), bf16[16,96,1280]{2,1,0:T(8,128)(2,1)}, u32[]{:S(2)}, u32[]{:S(2)}) %all-to-all-start.3) | async-done | bytes 3932192 | tf_op jit(solution)/shard_map/all_to_all | solution.py:809
  507.9 4.1 reduce-scatter.5.cloned.1.call-done
  520.8 4.3 all-to-all-start.4
  526.0 20.6 %all-to-all-done.4 = bf16[8,12,6400]{2,1,0:T(8,128)(2,1)S(1)} async-done(((bf16[8,12,6400]{2,1,0:T(8,128)(2,1)}), bf16[8,12,6400]{2,1,0:T(8,128)(2,1)S(1)}, u32[]{:S(2)}, u32[]{:S(2)}) %all-to-all-start.4) | async-done | bytes 1228832 | tf_op jit(solution)/shard_map/all_to_all | solution.py:568
  (476 shorter events, 206.8 us)
Async XLA Ops:
  7.2 97.3 %all-gather.5.cloned.1.call-start = ((), (), s32[]{:S(2)}) async-start(), calls=%async_computation.7 | async-start | bytes 6266880 | tf_op jit(solution)/shard_map/all_gather | solution.py:614
  28.1 141.2 %all-gather.7.cloned.1.call-start = ((), (), s32[]{:S(2)}) async-start(), calls=%async_computation.8 | async-start | bytes 10027008 | tf_op jit(solution)/shard_map/all_gather | solution.py:625
  61.9 186.2 %all-gather.9.cloned.1.call-start = ((), (), s32[]{:S(2)}) async-start(), calls=%async_computation.11 | async-start | bytes 8355840 | tf_op jit(solution)/shard_map/all_gather | solution.py:678
  61.9 17.2 %collective-permute-start.2 = (f32[1,6,1536]{2,0,1:T(1,128)S(1)}, f32[1,6,1536]{2,0,1:T(1,128)S(1)}, u32[]{:S(2)}, u32[]{:S(2)}) collective-permute-start(f32[1,6,1536]{2,0,1:T(1,128)S(1)} %copy-done.45), channel_id=1, source_target_pairs={{0,2},{2,0},{1,3},{3,1},{4,6},{6,4},{5,7},{7,5},{8,10},{10,8},{9,1... | collective-permute-start | bytes 110600 | tf_op jit(solution)/shard_map/ppermute | solution.py:40
  63.2 16.1 %collective-permute-start = (bf16[128,1536]{1,0:T(8,128)(2,1)S(1)}, bf16[128,1536]{1,0:T(8,128)(2,1)S(1)}, u32[]{:S(2)}, u32[]{:S(2)}) collective-permute-start(bf16[128,1536]{1,0:T(8,128)(2,1)S(1)} %bitcast.240), channel_id=1, source_target_pairs={{0,1},{1,0},{2,3},{3,2},{4,5},{5,4},{6,7},{7,6},{8,9},{9,8},{10,11... | collective-permute-start | bytes 1179656 | tf_op jit(solution)/shard_map/ppermute | solution.py:40
  63.5 14.5 %collective-permute-start.11 = (bf16[128,768]{1,0:T(8,128)(2,1)S(1)}, bf16[128,768]{1,0:T(8,128)(2,1)S(1)}, u32[]{:S(2)}, u32[]{:S(2)}) collective-permute-start(bf16[128,768]{1,0:T(8,128)(2,1)S(1)} %get-tuple-element.313), channel_id=1, source_target_pairs={{0,2},{2,0},{1,3},{3,1},{4,6},{6,4},{5,7},{7,5},{8,10},{10,8},{9,1... | collective-permute-start | bytes 589832 | tf_op jit(solution)/shard_map/ppermute | solution.py:40
  64.0 15.0 %collective-permute-start.12 = (bf16[128,768]{1,0:T(8,128)(2,1)S(1)}, bf16[128,768]{1,0:T(8,128)(2,1)S(1)}, u32[]{:S(2)}, u32[]{:S(2)}) collective-permute-start(bf16[128,768]{1,0:T(8,128)(2,1)S(1)} %get-tuple-element.311), channel_id=1, source_target_pairs={{0,2},{2,0},{1,3},{3,1},{4,6},{6,4},{5,7},{7,5},{8,10},{10,8},{9,1... | collective-permute-start | bytes 589832 | tf_op jit(solution)/shard_map/ppermute | solution.py:40
  75.6 18.8 %collective-permute-start.9 = (bf16[256,1536]{1,0:T(8,128)(2,1)S(1)}, bf16[256,1536]{1,0:T(8,128)(2,1)S(1)}, u32[]{:S(2)}, u32[]{:S(2)}) collective-permute-start(bf16[256,1536]{1,0:T(8,128)(2,1)S(1)} %bitcast.264), channel_id=1, source_target_pairs={{0,1},{1,0},{2,3},{3,2},{4,5},{5,4},{6,7},{7,6},{8,9},{9,8},{10,11... | collective-permute-start | bytes 2359304 | tf_op jit(solution)/shard_map/ppermute | solution.py:40
  79.4 17.9 %collective-permute-start.1 = (bf16[256,1536]{1,0:T(8,128)(2,1)S(1)}, bf16[256,1536]{1,0:T(8,128)(2,1)S(1)}, u32[]{:S(2)}, u32[]{:S(2)}) collective-permute-start(bf16[256,1536]{1,0:T(8,128)(2,1)S(1)} %maximum_select_fusion.3), channel_id=1, source_target_pairs={{0,2},{2,0},{1,3},{3,1},{4,6},{6,4},{5,7},{7,5},{8,10},{10,8},{9,1... | collective-permute-start | bytes 2359304 | tf_op jit(solution)/shard_map/ppermute | solution.py:40
  113.9 13.5 %collective-permute-start.15 = (f32[2,512]{0,1:T(8,128)S(1)}, f32[2,512]{0,1:T(8,128)S(1)}, u32[]{:S(2)}, u32[]{:S(2)}) collective-permute-start(f32[2,512]{0,1:T(8,128)S(1)} %bitcast.262), channel_id=1, source_target_pairs={{0,3},{3,0},{1,2},{2,1},{4,7},{7,4},{5,6},{6,5},{8,11},{11,8},{9,1... | collective-permute-start | bytes 12296 | tf_op jit(solution)/shard_map/ppermute | solution.py:78
  157.4 224.3 %reduce-scatter.3.cloned.1.call-start = ((), (), s32[]{:S(2)}) async-start(), calls=%async_computation.9 | async-start | bytes 8355840 | tf_op jit(solution)/shard_map/reduce_scatter | solution.py:730
  165.3 10.5 %collective-permute-start.22 = (bf16[256,768]{1,0:T(8,128)(2,1)S(1)}, bf16[256,768]{1,0:T(8,128)(2,1)S(1)}, u32[]{:S(2)}, u32[]{:S(2)}) collective-permute-start(bf16[256,768]{1,0:T(8,128)(2,1)S(1)} %fusion.32), channel_id=1, source_target_pairs={{0,1},{1,0},{4,5},{5,4},{2,3},{3,2},{6,7},{7,6},{8,9},{9,8},{12,13... | collective-permute-start | bytes 1179656 | tf_op jit(solution)/shard_map/ppermute | solution.py:46
  165.5 19.3 %collective-permute-start.23 = (bf16[256,768]{1,0:T(8,128)(2,1)S(1)}, bf16[256,768]{1,0:T(8,128)(2,1)}, u32[]{:S(2)}, u32[]{:S(2)}) collective-permute-start(bf16[256,768]{1,0:T(8,128)(2,1)S(1)} %fusion.32), channel_id=1, source_target_pairs={{0,4},{1,5},{4,0},{5,1},{2,6},{3,7},{6,2},{7,3},{8,12},{9,13},{12,... | collective-permute-start | bytes 1179656 | tf_op jit(solution)/shard_map/ppermute | solution.py:46
  167.3 19.6 %collective-permute-start.24 = (bf16[256,768]{1,0:T(8,128)(2,1)S(1)}, bf16[256,768]{1,0:T(8,128)(2,1)}, u32[]{:S(2)}, u32[]{:S(2)}) collective-permute-start(bf16[256,768]{1,0:T(8,128)(2,1)S(1)} %fusion.32), channel_id=1, source_target_pairs={{0,5},{1,4},{4,1},{5,0},{2,7},{3,6},{6,3},{7,2},{8,13},{9,12},{12,... | collective-permute-start | bytes 1179656 | tf_op jit(solution)/shard_map/ppermute | solution.py:46
  187.1 11.9 %collective-permute-start.25 = (f32[1,256]{1,0:T(1,128)S(1)}, f32[1,256]{1,0:T(1,128)S(1)}, u32[]{:S(2)}, u32[]{:S(2)}) collective-permute-start(f32[1,256]{1,0:T(1,128)S(1)} %bitcast.314), channel_id=1, source_target_pairs={{0,2},{2,0},{1,3},{3,1},{4,6},{6,4},{5,7},{7,5},{8,10},{10,8},{9,1... | collective-permute-start | bytes 3080 | tf_op jit(solution)/shard_map/ppermute | solution.py:40
  220.0 10.7 %collective-permute-start.29 = (bf16[256,768]{1,0:T(8,128)(2,1)S(1)}, bf16[256,768]{1,0:T(8,128)(2,1)S(1)}, u32[]{:S(2)}, u32[]{:S(2)}) collective-permute-start(bf16[256,768]{1,0:T(8,128)(2,1)S(1)} %fusion.36), channel_id=1, source_target_pairs={{0,1},{1,0},{4,5},{5,4},{2,3},{3,2},{6,7},{7,6},{8,9},{9,8},{12,13... | collective-permute-start | bytes 1179656 | tf_op jit(solution)/shard_map/ppermute | solution.py:46
  220.1 19.8 %collective-permute-start.30 = (bf16[256,768]{1,0:T(8,128)(2,1)S(1)}, bf16[256,768]{1,0:T(8,128)(2,1)S(1)}, u32[]{:S(2)}, u32[]{:S(2)}) collective-permute-start(bf16[256,768]{1,0:T(8,128)(2,1)S(1)} %fusion.36), channel_id=1, source_target_pairs={{0,4},{1,5},{4,0},{5,1},{2,6},{3,7},{6,2},{7,3},{8,12},{9,13},{12,... | collective-permute-start | bytes 1179656 | tf_op jit(solution)/shard_map/ppermute | solution.py:46
  222.3 19.5 %collective-permute-start.31 = (bf16[256,768]{1,0:T(8,128)(2,1)S(1)}, bf16[256,768]{1,0:T(8,128)(2,1)S(1)}, u32[]{:S(2)}, u32[]{:S(2)}) collective-permute-start(bf16[256,768]{1,0:T(8,128)(2,1)S(1)} %fusion.36), channel_id=1, source_target_pairs={{0,5},{1,4},{4,1},{5,0},{2,7},{3,6},{6,3},{7,2},{8,13},{9,12},{12,... | collective-permute-start | bytes 1179656 | tf_op jit(solution)/shard_map/ppermute | solution.py:46
  226.1 18.9 %collective-permute-start.33 = (bf16[1024,768]{1,0:T(8,128)(2,1)S(1)}, bf16[1024,768]{1,0:T(8,128)(2,1)S(1)}, u32[]{:S(2)}, u32[]{:S(2)}) collective-permute-start(bf16[1024,768]{1,0:T(8,128)(2,1)S(1)} %constant_dynamic-update-slice_fusion.g_ref), channel_id=1, source_target_pairs={{0,2},{2,0},{1,3},{3,1},{4,6},{6,4},{5,7},{7,5},{8,10},{10,8},{9,1... | collective-permute-start | bytes 4718600 | tf_op jit(solution)/shard_map/ppermute | solution.py:40
  282.2 229.9 %reduce-scatter.5.cloned.1.call-start = ((), (), s32[]{:S(2)}) async-start(), calls=%async_computation.10 | async-start | bytes 12533760 | tf_op jit(solution)/shard_map/reduce_scatter | solution.py:777
  291.5 31.7 %collective-permute-start.40 = (bf16[1024,768]{1,0:T(8,128)(2,1)S(1)}, bf16[1024,768]{1,0:T(8,128)(2,1)S(1)}, u32[]{:S(2)}, u32[]{:S(2)}) collective-permute-start(bf16[1024,768]{1,0:T(8,128)(2,1)S(1)} %broadcast_select_fusion), channel_id=1, source_target_pairs={{0,2},{2,0},{1,3},{3,1},{4,6},{6,4},{5,7},{7,5},{8,10},{10,8},{9,1... | collective-permute-start | bytes 4718600 | tf_op jit(solution)/shard_map/ppermute | solution.py:40
  293.3 10.7 %collective-permute-start.35 = (bf16[256,768]{1,0:T(8,128)(2,1)S(1)}, bf16[256,768]{1,0:T(8,128)(2,1)S(1)}, u32[]{:S(2)}, u32[]{:S(2)}) collective-permute-start(bf16[256,768]{1,0:T(8,128)(2,1)S(1)} %get-tuple-element.289), channel_id=1, source_target_pairs={{0,1},{1,0},{4,5},{5,4},{2,3},{3,2},{6,7},{7,6},{8,9},{9,8},{12,13... | collective-permute-start | bytes 1179656 | tf_op jit(solution)/shard_map/ppermute | solution.py:72
  293.4 20.3 %collective-permute-start.36 = (bf16[256,768]{1,0:T(8,128)(2,1)S(1)}, bf16[256,768]{1,0:T(8,128)(2,1)S(1)}, u32[]{:S(2)}, u32[]{:S(2)}) collective-permute-start(bf16[256,768]{1,0:T(8,128)(2,1)S(1)} %get-tuple-element.291), channel_id=1, source_target_pairs={{0,4},{1,5},{4,0},{5,1},{2,6},{3,7},{6,2},{7,3},{8,12},{9,13},{12,... | collective-permute-start | bytes 1179656 | tf_op jit(solution)/shard_map/ppermute | solution.py:72
  296.1 19.7 %collective-permute-start.37 = (bf16[256,768]{1,0:T(8,128)(2,1)S(1)}, bf16[256,768]{1,0:T(8,128)(2,1)S(1)}, u32[]{:S(2)}, u32[]{:S(2)}) collective-permute-start(bf16[256,768]{1,0:T(8,128)(2,1)S(1)} %get-tuple-element.290), channel_id=1, source_target_pairs={{0,5},{1,4},{4,1},{5,0},{2,7},{3,6},{6,3},{7,2},{8,13},{9,12},{12,... | collective-permute-start | bytes 1179656 | tf_op jit(solution)/shard_map/ppermute | solution.py:72
  326.6 22.2 %collective-permute-start.41 = (bf16[256,768]{1,0:T(8,128)(2,1)}, bf16[256,768]{1,0:T(8,128)(2,1)S(1)}, u32[]{:S(2)}, u32[]{:S(2)}) collective-permute-start(bf16[256,768]{1,0:T(8,128)(2,1)} %get-tuple-element.91), channel_id=1, source_target_pairs={{0,1},{1,0},{4,5},{5,4},{2,3},{3,2},{6,7},{7,6},{8,9},{9,8},{12,13... | collective-permute-start | bytes 1179656 | tf_op jit(solution)/shard_map/ppermute | solution.py:746
  326.7 22.3 %collective-permute-start.42 = (bf16[256,768]{1,0:T(8,128)(2,1)}, bf16[256,768]{1,0:T(8,128)(2,1)}, u32[]{:S(2)}, u32[]{:S(2)}) collective-permute-start(bf16[256,768]{1,0:T(8,128)(2,1)} %get-tuple-element.92), channel_id=1, source_target_pairs={{0,4},{1,5},{4,0},{5,1},{2,6},{3,7},{6,2},{7,3},{8,12},{9,13},{12,... | collective-permute-start | bytes 1179656 | tf_op jit(solution)/shard_map/ppermute | solution.py:746
  328.9 20.0 %collective-permute-start.43 = (bf16[256,768]{1,0:T(8,128)(2,1)}, bf16[256,768]{1,0:T(8,128)(2,1)}, u32[]{:S(2)}, u32[]{:S(2)}) collective-permute-start(bf16[256,768]{1,0:T(8,128)(2,1)} %get-tuple-element.93), channel_id=1, source_target_pairs={{0,5},{1,4},{4,1},{5,0},{2,7},{3,6},{6,3},{7,2},{8,13},{9,12},{12,... | collective-permute-start | bytes 1179656 | tf_op jit(solution)/shard_map/ppermute | solution.py:746
  365.9 10.1 %collective-permute-start.47 = (f32[2,256]{1,0:T(2,128)S(1)}, f32[2,256]{1,0:T(2,128)S(1)}, u32[]{:S(2)}, u32[]{:S(2)}) collective-permute-start(f32[2,256]{1,0:T(2,128)S(1)} %pad_maximum_fusion.14), channel_id=1, source_target_pairs={{0,2},{2,0},{1,3},{3,1},{4,6},{6,4},{5,7},{7,5},{8,10},{10,8},{9,1... | collective-permute-start | bytes 6152 | tf_op jit(solution)/shard_map/ppermute | solution.py:40
  407.4 12.2 %collective-permute-start.54 = (f32[2,512]{0,1:T(8,128)}, f32[2,512]{0,1:T(8,128)}, u32[]{:S(2)}, u32[]{:S(2)}) collective-permute-start(f32[2,512]{0,1:T(8,128)} %bitcast.275), channel_id=1, source_target_pairs={{0,3},{3,0},{1,2},{2,1},{4,7},{7,4},{5,6},{6,5},{8,11},{11,8},{9,1... | collective-permute-start | bytes 12296 | tf_op jit(solution)/shard_map/ppermute | solution.py:78
  433.7 74.3 %all-to-all-start.3 = ((bf16[16,96,1280]{2,1,0:T(8,128)(2,1)}), bf16[16,96,1280]{2,1,0:T(8,128)(2,1)}, u32[]{:S(2)}, u32[]{:S(2)}) async-start(bf16[16,96,1280]{2,1,0:T(8,128)(2,1)} %bitcast.248), calls=%async_computation.4 | async-start | bytes 7864320 | tf_op jit(solution)/shard_map/all_to_all | solution.py:809
  441.0 10.9 %collective-permute-start.56 = (bf16[128,1536]{1,0:T(8,128)(2,1)S(1)}, bf16[128,1536]{1,0:T(8,128)(2,1)S(1)}, u32[]{:S(2)}, u32[]{:S(2)}) collective-permute-start(bf16[128,1536]{1,0:T(8,128)(2,1)S(1)} %select_convert_fusion), channel_id=1, source_target_pairs={{0,1},{1,0},{2,3},{3,2},{4,5},{5,4},{6,7},{7,6},{8,9},{9,8},{10,11... | collective-permute-start | bytes 1179656 | tf_op jit(solution)/shard_map/ppermute | solution.py:40
  520.8 25.8 %all-to-all-start.4 = ((bf16[8,12,6400]{2,1,0:T(8,128)(2,1)}), bf16[8,12,6400]{2,1,0:T(8,128)(2,1)S(1)}, u32[]{:S(2)}, u32[]{:S(2)}) async-start(bf16[8,12,6400]{2,1,0:T(8,128)(2,1)} %reshape.486), calls=%async_computation.6 | async-start | bytes 3276800 | tf_op jit(solution)/shard_map/all_to_all | solution.py:568
  (88 other events, 988.6 us)
Sparse Core Ops, SparseCore 0:
  28.2 59.3 all-gather.4
  89.7 75.2 all-gather.6
  167.8 68.1 all-gather.8
  282.3 79.5 reduce-scatter.2
  381.9 130.0 reduce-scatter.4

commit v2 on v1

--- a/solution.py
+++ b/solution.py
@@ -62,15 +62,6 @@
 
 def axis_join(piece, axis_name, dim=0):
     return jnp.concatenate(in_order(others(piece, axis_name), lax.axis_index(axis_name)), dim)
-
-
-def near_sum(blocks, axis_name):
-    size = lax.axis_size(axis_name)
-    total = blocks[0].astype(f32)
-    for k in range(1, size):
-        pairs = [(i, i ^ k) for i in range(size)]
-        total = total + lax.ppermute(blocks[k], axis_name, pairs).astype(f32)
-    return total
 
 
 def group_sum(small):
@@ -501,42 +492,61 @@
     )(core, *inputs, grad_hidden, activated, *grads)
 
 
-def tail_kernel(core_ref, x_ref, g_ref, w_ref, n_ref, small_ref, lines_ref, keep_ref, give_ref):
-    cols, some = g_ref.shape[1], x_ref.shape[0] // 2
+def tail_kernel(places, at_ref, x_ref, g_ref, w_ref, n_ref, small_ref, first_ref, second_ref, keep_ref, give_ref, held):
+    cut, some = first_ref.shape[1], x_ref.shape[0] // 2
     ones = jnp.ones((x_ref.shape[0], 128), bf16)
     part = mm_nt(g_ref[...], w_ref[...])
     low = part.astype(bf16)
-    first = mm_tn(low, ones)
-    second = mm_tn((part * n_ref[...].astype(f32)).astype(bf16), ones)
-    lane = lax.broadcasted_iota(jnp.int32, first.shape, 1)
-    small = jnp.where(lane == 6, first, jnp.where(lane == 7, second, small_ref[...]))
-    lines_ref[:, cols:] = small.astype(bf16)
-    zero = core_ref[0] == 0
+    shift = mm_tn(low, ones)
+    scale = mm_tn((part * n_ref[...].astype(f32)).astype(bf16), ones)
+    lane = lax.broadcasted_iota(jnp.int32, shift.shape, 1)
+    small = jnp.where(lane == 6, shift, jnp.where(lane == 7, scale, small_ref[...]))
+    held[...] = small.astype(bf16)
+    zero = at_ref[0] == 0
     keep_ref[...] = jnp.where(zero, low[:some], low[some:])
     give_ref[...] = jnp.where(zero, low[some:], low[:some])
-    half = x_ref.shape[1] // 2
+    down, across = places
+    lines = x_ref.shape[1] // (down * across)
+    step = down * across // 2
     for k in range(2):
-        rows = pl.ds(k * half, half)
-        lines_ref[rows, :cols] = mm_tn(x_ref[:, rows], g_ref[...]).astype(bf16)
-
-
-def tail(core, inputs, grad, weight, norm, small):
+        rows = pl.ds(k * step * lines, step * lines)
+        grad = mm_tn(x_ref[:, rows], g_ref[...]).astype(bf16)
+        for i in range(step):
+            y, x = divmod(k * step + i, across)
+            y = y ^ at_ref[1]
+            here = slice(i * lines, (i + 1) * lines)
+            there = pl.ds(pl.multiple_of((x * down + y) * lines, 16), lines)
+            first_ref[there, :] = grad[here, :cut]
+            there = pl.ds(pl.multiple_of((y * across + x) * lines, 16), lines)
+            second_ref[there, : g_ref.shape[1] - cut] = grad[here, cut:]
+            second_ref[there, g_ref.shape[1] - cut :] = held[pl.ds((k * step + i) * lines, lines), :]
+
+
+def tail(places, at, inputs, grad, weight, norm, small):
     rows, width = inputs.shape
+    cut = (grad.shape[1] + 128) // 2
     out = [
-        jax.ShapeDtypeStruct((width, grad.shape[1] + 128), bf16),
+        jax.ShapeDtypeStruct((width, cut), bf16),
+        jax.ShapeDtypeStruct((width, cut), bf16),
         jax.ShapeDtypeStruct((rows // 2, width), bf16),
         jax.ShapeDtypeStruct((rows // 2, width), bf16),
     ]
-    vmem = pl.BlockSpec(memory_space=pltpu.VMEM)
+
+    def first_block(shape):
+        return pl.BlockSpec(shape, lambda i: (0, 0))
+
     return pl.pallas_call(
-        tail_kernel,
-        in_specs=[pl.BlockSpec(memory_space=pltpu.SMEM)] + [vmem] * 5,
-        out_specs=[vmem] * 3,
+        functools.partial(tail_kernel, places),
+        grid=(1,),
+        in_specs=[pl.BlockSpec(memory_space=pltpu.SMEM)]
+        + [first_block(s) for s in (inputs.shape, grad.shape, (width, grad.shape[1]), norm.shape, small.shape)],
+        out_specs=[first_block(o.shape) for o in out],
         out_shape=out,
+        scratch_shapes=[pltpu.VMEM((width, 128), bf16)],
         compiler_params=pltpu.CompilerParams(vmem_limit_bytes=56 * 2**20),
         cost_estimate=pl.CostEstimate(flops=8 * 10**9, bytes_accessed=10**7, transcendentals=0),
         name="tail",
-    )(core, inputs, grad, weight, norm, small)
+    )(at, inputs, grad, weight, norm, small)
 
 
 def inverse_freq(pair_total):
@@ -691,15 +701,15 @@
     cross_key = (ck_pre * inv_ck[:, None] * g_ck).astype(bf16)
     cross_value = ckv[:, half:].astype(bf16)
     cq_pre = mm(cross_input, cq_weight)
-    cq_pre, *grad_three = lax.optimization_barrier((cq_pre, *grad_three))
+    inv_cq = lax.rsqrt(core_sum(jnp.sum(cq_pre * cq_pre, axis=-1)[None]) / width + NORM_EPS)[0]
+    cross_query, cross_heads = cross_forward(cq_pre, inv_cq[:, None], g_cq, cross_key, cross_value)
+    cross_heads, *grad_three = lax.optimization_barrier((cross_heads, *grad_three))
 
     def both_cores(pieces):
         lines = jnp.concatenate(pieces, 0)
         return lines, swap(lines, "core")
 
     grad_three = both_cores(grad_three)
-    inv_cq = lax.rsqrt(core_sum(jnp.sum(cq_pre * cq_pre, axis=-1)[None]) / width + NORM_EPS)[0]
-    cross_query, cross_heads = cross_forward(cq_pre, inv_cq[:, None], g_cq, cross_key, cross_value)
     cross_tokens = join(cross_heads, "core", 1)
     after_cross = after_attn + mm(cross_tokens, co_weight)
 
@@ -711,12 +721,14 @@
         core_row, mlp_input, grad_three, mlp_pack, line_rows, hidden, hid_pad
     )
 
+    def to_near(blocks):
+        return [lax.ppermute(blocks[k], CHIPS, [(i, i ^ (k + 1)) for i in range(4)]) for k in range(3)]
+
     def core_lines(keep, give):
         lines = keep.astype(f32) + swap(give, "core").astype(f32)
         return lines[: 2 * tokens], jnp.split(lines[2 * tokens :].astype(bf16), 3, 0)
 
-    near, far = core_lines(keep, give)
-    grad_mlp_input = near_sum([near, *far], CHIPS)
+    near_input, far = core_lines(keep, give)
     down_weight = jnp.concatenate(
         [
             mlp_pack[:, at : at + hid_pad].reshape(hidden, PACK)
@@ -724,8 +736,12 @@
         ],
         axis=1,
     )
-    near, far = core_lines(*halves(mm(activated, down_weight).astype(bf16), "core", 1))
+    near, three = core_lines(*halves(mm(activated, down_weight).astype(bf16), "core", 1))
+    activated, grad_hidden, *far = lax.optimization_barrier((activated, grad_hidden, *far))
+    far = to_near(far)
     mlp_lines = mlp_grads(core_row, mlp_input, grad_hidden, activated, grad_three, peers)
+    mlp_lines, *far = lax.optimization_barrier((mlp_lines, *far))
+    grad_mlp_input = near_input + sum(part.astype(f32) for part in far)
     mlp_lines = mlp_lines.reshape(-1, PACK)
     mlp_sum = lax.psum_scatter(mlp_lines, PLACES, scatter_dimension=0, tiled=True)
 
@@ -742,11 +758,11 @@
 
     grad_heads = scatter_sum(mm_nt(grad_two, co_weight).astype(bf16), "core", 1).astype(bf16)
     rest_lines = tn_pack(cross_tokens, grad_two, 4, 5, peers)
-    grad_heads, near, *far = lax.optimization_barrier((grad_heads, near, *far))
-    far = [lax.ppermute(far[k], CHIPS, [(i, i ^ (k + 1)) for i in range(4)]) for k in range(3)]
+    grad_heads, near, *three = lax.optimization_barrier((grad_heads, near, *three))
+    three = to_near(three)
     up_cq, up_ck, up_cv = cross_backward(cross_query, cross_key, cross_value, grad_heads)
-    up_cq, *far = lax.optimization_barrier((up_cq, *far))
-    branch_three = near + sum(part.astype(f32) for part in far)
+    up_cq, *three = lax.optimization_barrier((up_cq, *three))
+    branch_three = near + sum(part.astype(f32) for part in three)
     result_here = (after_cross + branch_three * per_clip(5)).astype(bf16)
     grad_mod5 = jnp.sum(up_here * branch_three, axis=0)
     result = trade(result_here, "core", 0, 1)
@@ -803,12 +819,27 @@
         core == 0, jnp.pad(halfs, ((0, 0), (0, half))), jnp.pad(halfs, ((0, 0), (half, 0)))
     )
     small_cols = jnp.pad(smalls.T, ((0, 0), (0, 116)))
-    last_lines, keep, give = tail(
-        core_row, attn_input, grad_qkv, qkv_weight, norm_wide.astype(bf16), small_cols
-    )
-    last_parts = lax.all_to_all(
-        last_lines.reshape(peers, line_rows, -1), PLACES, split_axis=0, concat_axis=0, tiled=True
-    )
+    down_across = (lax.axis_size("y"), lax.axis_size("x"))
+    at_row = jnp.stack([core, lax.axis_index("y")]).astype(jnp.int32)
+    *last_lines, keep, give = tail(
+        down_across, at_row, attn_input, grad_qkv, first_weight, norm_wide.astype(bf16), small_cols
+    )
+
+    def sum_both(by_x, by_y):
+        by_x = by_x.reshape(down_across[1], -1, by_x.shape[-1])
+        by_y = jnp.split(by_y, down_across[0], 0)
+        from_x = lax.all_to_all(by_x, "x", split_axis=0, concat_axis=0, tiled=True)
+        from_y = [
+            lax.ppermute(by_y[k], "y", [(at, at ^ k) for at in range(down_across[0])])
+            for k in range(1, down_across[0])
+        ]
+        from_x, *from_y = lax.optimization_barrier((from_x, *from_y))
+        total = sum((part.astype(f32) for part in from_y), by_y[0].astype(f32))
+        return jnp.sum(from_x.astype(f32), axis=0).astype(bf16), total.astype(bf16)
+
+    last_first, last_second = sum_both(*last_lines)
+    last_second, last_first = sum_both(last_second, last_first)
+    last_parts = [last_first, last_second]
 
     grad_attn_input = keep.astype(f32) + swap(give, "core").astype(f32)
     grad_attn_input = scatter_sum(grad_attn_input, "zl", 0)
@@ -819,13 +850,12 @@
         - jnp.mean(scaled, axis=-1, keepdims=True)
         - norm_one * jnp.mean(scaled * norm_one, axis=-1, keepdims=True)
     )
-    mlp_sum, input_grad, last_parts, rest_sum = lax.optimization_barrier(
-        (mlp_sum, input_grad, last_parts, rest_sum)
+    mlp_sum, input_grad, rest_sum, *last_parts = lax.optimization_barrier(
+        (mlp_sum, input_grad, rest_sum, *last_parts)
     )
     up_lines = line_rows * (hidden // PACK)
-    last_sum = jnp.sum(last_parts.astype(f32), axis=0).astype(bf16)
     rest = jnp.concatenate(
-        jnp.split(rest_sum, 5, 0) + [last_sum] + jnp.split(mlp_sum[:up_lines], hidden // PACK, 0), axis=1
+        jnp.split(rest_sum, 5, 0) + last_parts + jnp.split(mlp_sum[:up_lines], hidden // PACK, 0), axis=1
     )
     lines = along_line(rest.reshape(8, rows_each, -1))
     up_rows = lines[..., -hidden:].reshape(8, rows_each, peers, hid_pad)[..., :hid_each]

time: 570 us -> 542 us (0.951)
  waiting for transfers between devices: 203 us -> 146 us
  starting transfers between devices: 60.3 us -> 78.7 us
  other arithmetic: 56.2 us -> 66.1 us
    all_to_all x1 -> x2, waiting for transfers between devices: 54.4 us -> 0.01 us  [sum_both(): from_x = lax.all_to_all(by_x, 'x', split_axis=0, concat_axis=0, tiled=True)]
    ppermute x12, waiting for transfers between devices: 35.7 us -> 21.3 us  [others(): lax.ppermute(array, axis_name, [(i, i ^ k) for i in range(size)])]
    ppermute x6 -> x12, waiting for transfers between devices: 18.6 us -> 27.2 us  [the longest x6 22.1 us: sum_both(): lax.ppermute(by_y[k], 'y', [(at, at ^ k) for at in range(down_across[0])])]
    ppermute x6 -> x12, starting transfers between devices: 7.94 us -> 15 us  [the longest x6 8.33 us: to_near(): lax.ppermute(blocks[k], CHIPS, [(i, i ^ k + 1) for i in range(4)])]
    all_gather x1, waiting for transfers between devices: 0.01 us -> 6.25 us  [on_device(): mlp_pack = lax.all_gather(mlp_shard, PLACES, axis=0)]
    unnamed x149 -> x158, local copies, waits for them, and re-layouts: 16.6 us -> 18.7 us
  transfers between devices with their start and end apart: 64 -> 71, of which waited for: 34 -> 34; matrix products, arithmetic and copies ran while one was open for 19% -> 21% of each run, Pallas kernels for 12% -> 15%
where the time goes in v2:
time: 542 us; the launch traced here: 533 us
  waiting for transfers between devices  146 us (27%)
  Pallas kernels  100 us (18%)
  starting transfers between devices  78.7 us (15%)
  other arithmetic  66.1 us (12%)
  local copies, waits for them, and re-layouts  45.6 us (8%)
  blocking collectives  45.2 us (8%)
  matrix products  34.4 us (6%)
  between operations  16.3 us (3%)
    ppermute x37, waiting for transfers between devices, swap(): return lax.ppermute(array, axis_name, SWAP)  54.1 us
    all_to_all x3, blocking collectives, along_line(): return lax.all_to_all(parts, LINE, split_axis=0, concat_axis=0, tiled=True)  45.2 us
    ppermute x37, starting transfers between devices, swap(): return lax.ppermute(array, axis_name, SWAP)  32 us
    dot_general x6, matrix products, mm(): return jnp.dot(left, right, preferred_element_type=f32)  26.6 us
    ppermute x6, waiting for transfers between devices, sum_both(): lax.ppermute(by_y[k], 'y', [(at, at ^ k) for at in range(down_across[0])])  22.1 us
    ppermute x12, waiting for transfers between devices, others(): lax.ppermute(array, axis_name, [(i, i ^ k) for i in range(size)])  21.3 us
    all_to_all x1, waiting for transfers between devices, along_line(): return lax.all_to_all(parts, LINE, split_axis=0, concat_axis=0, tiled=True)  20.6 us
    pallas_call x4, Pallas kernels, tn_pack(): pl.pallas_call(functools.partial(tn_pack_kernel, place), in_specs=[vmem,...  20.2 us
  transfers between devices with their start and end apart: 71, of which 34 were waited for; matrix products, arithmetic and copies ran while one was open for 21% of the time, Pallas kernels for 15%

profile of v2, /device:TPU:1, one launch (start us, length us, event | category | flops | bytes accessed | tf_op | source)
XLA Modules:
  0.0 532.8 jit_solution(5808369217899332529)
XLA Ops:
  11.4 15.8 %all_to_all.30 = bf16[8,12,2048]{2,1,0:T(8,128)(2,1)S(1)} all-to-all(bf16[8,12,2048]{2,1,0:T(8,128)(2,1)S(1)} %copy.187), channel_id=1, replica_groups=mesh['y'=4,'x'=4,'zh'=2,'core'=2,'zl'=2] {'zh','core','zl'}, dimensions={0} | all-to-all | bytes 786432 | tf_op jit(solution)/shard_map/all_to_all | solution.py:578
  44.5 18.7 %all_to_all.31 = bf16[8,12,3072]{2,1,0:T(8,128)(2,1)S(1)} all-to-all(bf16[8,12,3072]{2,1,0:T(8,128)(2,1)S(1)} %pad_maximum_fusion.3), channel_id=1, replica_groups=mesh['y'=4,'x'=4,'zh'=2,'core'=2,'zl'=2] {'zh','core','zl'}, dimensions={0} | all-to-all | bytes 1179648 | tf_op jit(solution)/shard_map/all_to_all | solution.py:578
  78.9 14.5 %collective-permute-done.9 = bf16[256,1536]{1,0:T(8,128)(2,1)S(1)} collective-permute-done((bf16[256,1536]{1,0:T(8,128)(2,1)S(1)}, bf16[256,1536]{1,0:T(8,128)(2,1)S(1)}, u32[]{:S(2)}, u32[]{:S(2)}) %collective-permute-start.9) | collective-permute-done | bytes 786464 | tf_op jit(solution)/shard_map/ppermute | solution.py:40
  97.7 3.8 fusion.4
  103.7 6.5 %fusion.91 = (f32[512,1152]{1,0:T(8,128)}, f32[512,1152]{1,0:T(8,128)}) fusion(bf16[512,1536]{1,0:T(8,128)(2,1)S(1)} %get-tuple-element.88.x_ref, bf16[1536,1920]{1,0:T(8,128)(2,1)} %all-gather.5.cloned.1.call-done.w_ref), kind=kOutput, calls=%fused_computation.338 | convolution fusion | flops 1812529152 | bytes 9830400 | tf_op jit(solution)/shard_map/dot_general | solution.py:28
  115.1 6.2 %collective-permute-done.15 = f32[2,512]{0,1:T(8,128)S(1)} collective-permute-done((f32[2,512]{0,1:T(8,128)S(1)}, f32[2,512]{0,1:T(8,128)S(1)}, u32[]{:S(2)}, u32[]{:S(2)}) %collective-permute-start.15) | collective-permute-done | bytes 4128 | tf_op jit(solution)/shard_map/ppermute | solution.py:69
  121.3 5.5 %collective-permute-done.13 = f32[2,512]{0,1:T(8,128)S(1)} collective-permute-done((f32[2,512]{0,1:T(8,128)S(1)}, f32[2,512]{0,1:T(8,128)S(1)}, u32[]{:S(2)}, u32[]{:S(2)}) %collective-permute-start.13) | collective-permute-done | bytes 4128 | tf_op jit(solution)/shard_map/ppermute | solution.py:40
  127.6 7.4 %self_forward.1 = (bf16[512,384]{1,0:T(8,128)(2,1)}, bf16[512,384]{1,0:T(8,128)(2,1)}, bf16[512,384]{1,0:T(8,128)(2,1)}, bf16[512,384]{1,0:T(8,128)(2,1)}) custom-call(f32[512,1152]{1,0:T(8,128)} %get-tuple-element.395.q_ref.k_ref.v_ref, f32[512,1152]{1,0:T(8,128)} %get-tuple-element.395.q_ref.k_ref.v_ref, f32[512,1152]{1,0:T(8,128)} %get-tuple-element.395.q_ref.k_ref.v_ref, ...), custom_call_target="tpu_custom_call" | custom-call | flops 8000000000 | bytes 10000000 | tf_op jit(solution)/shard_map/self_forward/pallas_call | solution.py:182
  137.2 4.8 collective-permute-done.18
  145.7 10.8 %all_to_all.32 = bf16[8,12,1280]{2,1,0:T(8,128)(2,1)S(1)} all-to-all(bf16[8,12,1280]{2,1,0:T(8,128)(2,1)S(1)} %copy.196), channel_id=1, replica_groups=mesh['y'=4,'x'=4,'zh'=2,'core'=2,'zl'=2] {'zh','core','zl'}, dimensions={0} | all-to-all | bytes 491520 | tf_op jit(solution)/shard_map/all_to_all | solution.py:578
  172.6 6.9 %fusion = f32[1024,1536]{1,0:T(8,128)S(1)} fusion(bf16[1024,1536]{1,0:T(8,128)(2,1)S(1)} %copy-done.3, bf16[1536,3072]{1,0:T(8,128)(2,1)} %all-gather.7.cloned.1.call-done), kind=kOutput, calls=%fused_computation | convolution fusion | flops 4831838208 | bytes 14155776 | tf_op jit(solution)/shard_map/dot_general | solution.py:28
  187.2 7.8 %cross_forward.1 = (bf16[256,768]{1,0:T(8,128)(2,1)}, bf16[256,768]{1,0:T(8,128)(2,1)}) custom-call(f32[256,768]{1,0:T(8,128)} %get-tuple-element.397.q_ref, f32[256,1]{1,0:T(8,128)} %copy.195.r_ref, f32[1,768]{1,0:T(1,128)} %get-tuple-element.300.g_ref, bf16[1024,768]{1,0:T(8,128)(2,1)} %multiply_convert_fusion.1.k_ref, bf16[1024,768]{1,0:T(8,128)(2,1)} %slice.601.v_ref), custom_call_target="tpu_custom_call" | custom-call | flops 8999999488 | bytes 10000000 | tf_op jit(solution)/shard_map/cross_forward/pallas_call | solution.py:263
  209.6 13.8 %collective-permute-done.31 = bf16[256,768]{1,0:T(8,128)(2,1)S(1)} collective-permute-done((bf16[256,768]{1,0:T(8,128)(2,1)S(1)}, bf16[256,768]{1,0:T(8,128)(2,1)S(1)}, u32[]{:S(2)}, u32[]{:S(2)}) %collective-permute-start.31) | collective-permute-done | bytes 393248 | tf_op jit(solution)/shard_map/ppermute | solution.py:46
  229.5 6.3 %all-gather.9.cloned.1.call-done = bf16[15360,256]{1,0:T(8,128)(2,1)} async-done(((bf16[960,256]{1,0:T(8,128)(2,1)}), bf16[15360,256]{1,0:T(8,128)(2,1)}) %all-gather.9.cloned.1.call-update) | async-done | bytes 7864336 | tf_op jit(solution)/shard_map/all_gather | solution.py:688
  235.8 19.3 %mlp.1 = (bf16[1024,1280]{1,0:T(8,128)(2,1)}, bf16[1024,1280]{1,0:T(8,128)(2,1)}, bf16[1024,768]{1,0:T(8,128)(2,1)}, bf16[1024,768]{1,0:T(8,128)(2,1)}) custom-call(s32[1]{0:T(128)} %bitcast.47.core_ref, bf16[1024,768]{1,0:T(8,128)(2,1)} %copy-done.25, bf16[1024,768]{1,0:T(8,128)(2,1)} %collective-permute-done.32.xo_ref, bf16[1024,768]{1,0:T(8,128)(2,1)} %copy-done.51, ...), custom_call_target="tpu_custom_call" | custom-call | flops 12079595520 | bytes 7864320 | tf_op jit(solution)/shard_map/mlp/pallas_call | solution.py:374
  267.0 14.3 %mlp_grads.1 = bf16[16,960,256]{2,1,0:T(8,128)(2,1)} custom-call(s32[1]{0:T(128)} %bitcast.47.core_ref, bf16[1024,768]{1,0:T(8,128)(2,1)} %copy-done.25, bf16[1024,768]{1,0:T(8,128)(2,1)} %collective-permute-done.32.xo_ref, bf16[1024,1280]{1,0:T(8,128)(2,1)} %get-tuple-element.107.gh_ref, bf16[1024,1280]{1,0:T(8,128)(2,1)} %get-tuple-element.108.act_ref, ...), custom_call_target="tpu_custom_call" | custom-call | flops 8053063680 | bytes 7864320 | tf_op jit(solution)/shard_map/mlp_grads/pallas_call | solution.py:476
  290.7 4.4 convolution_convert_fusion
  312.1 9.8 %cross_backward.1 = (f32[256,768]{1,0:T(8,128)}, f32[1024,768]{1,0:T(8,128)}, bf16[1024,768]{1,0:T(8,128)(2,1)}) custom-call(bf16[256,768]{1,0:T(8,128)(2,1)} %get-tuple-element.116.qn_ref, bf16[1024,768]{1,0:T(8,128)(2,1)} %multiply_convert_fusion.1.k_ref, bf16[1024,768]{1,0:T(8,128)(2,1)} %slice.601.v_ref, bf16[256,768]{1,0:T(8,128)(2,1)} %add_convert_fusion.2.do_ref), custom_call_target="tpu_custom_call" | custom-call | flops 11000000512 | bytes 10000000 | tf_op jit(solution)/shard_map/cross_backward/pallas_call | solution.py:291
  322.0 3.8 multiply_reduce_fusion
  347.0 9.5 %tn_pack.6.rest_0_ = bf16[16,480,768]{2,1,0:T(8,128)(2,1)} custom-call(bf16[1024,1536]{1,0:T(8,128)(2,1)} %maximum_select_fusion.x_ref, bf16[1024,1536]{1,0:T(8,128)(2,1)} %pad_maximum_fusion.g_ref, bf16[16,480,768]{2,1,0:T(8,128)(2,1)} %tn_pack.5.rest_0_), custom_call_target="tpu_custom_call", output_to_operand_aliasing={{}: (2, {})} | custom-call | flops 4831838208 | bytes 4718592 | tf_op jit(solution)/shard_map/tn_pack/pallas_call | solution.py:427
  358.6 3.6 tn_pack.7
  362.2 5.2 reduce-scatter.3.cloned.1.call-done
  381.9 10.3 %self_backward.1 = (f32[512,384]{1,0:T(8,128)}, f32[512,384]{1,0:T(8,128)}, bf16[512,384]{1,0:T(8,128)(2,1)}, f32[512,2]{1,0:T(8,128)}, f32[2,3,2,128]{3,2,1,0:T(2,128)}) custom-call(bf16[512,384]{1,0:T(8,128)(2,1)} %get-tuple-element.130.qr_ref, bf16[512,384]{1,0:T(8,128)(2,1)} %get-tuple-element.131.kr_ref, bf16[512,384]{1,0:T(8,128)(2,1)} %get-tuple-element.132.vb_ref, ...), custom_call_target="tpu_custom_call" | custom-call | flops 11000000512 | bytes 10000000 | tf_op jit(solution)/shard_map/self_backward/pallas_call | solution.py:232
  397.1 5.4 %collective-permute-done.54 = f32[2,512]{0,1:T(8,128)} collective-permute-done((f32[2,512]{0,1:T(8,128)}, f32[2,512]{0,1:T(8,128)}, u32[]{:S(2)}, u32[]{:S(2)}) %collective-permute-start.54) | collective-permute-done | bytes 4128 | tf_op jit(solution)/shard_map/ppermute | solution.py:69
  402.5 4.5 collective-permute-done.52
  410.5 11.1 %tail.1 = (bf16[1536,640]{1,0:T(8,128)(2,1)}, bf16[1536,640]{1,0:T(8,128)(2,1)}, bf16[256,1536]{1,0:T(8,128)(2,1)}, bf16[256,1536]{1,0:T(8,128)(2,1)}) custom-call(s32[2]{0:T(128)} %pad_add_fusion.at_ref, bf16[512,1536]{1,0:T(8,128)(2,1)} %copy-done.26, bf16[512,1152]{1,0:T(8,128)(2,1)} %pad_maximum_fusion.2.g_ref, ...), custom_call_target="tpu_custom_call" | custom-call | flops 8000000000 | bytes 10000000 | tf_op jit(solution)/shard_map/tail/pallas_call | solution.py:538
  437.5 4.1 collective-permute-done.56
  442.0 17.2 %collective-permute-done.59 = bf16[384,640]{1,0:T(8,128)(2,1)S(1)} collective-permute-done((bf16[384,640]{1,0:T(8,128)(2,1)S(1)}, bf16[384,640]{1,0:T(8,128)(2,1)S(1)}, u32[]{:S(2)}, u32[]{:S(2)}) %collective-permute-start.59) | collective-permute-done | bytes 491552 | tf_op jit(solution)/shard_map/ppermute | solution.py:833
  464.5 4.8 all-to-all-start.4
  475.0 4.9 collective-permute-done.62
  487.8 5.6 %all-to-all-start.5 = ((bf16[8,12,6400]{2,1,0:T(8,128)(2,1)}), bf16[8,12,6400]{2,1,0:T(8,128)(2,1)S(1)}, u32[]{:S(2)}, u32[]{:S(2)}) async-start(bf16[8,12,6400]{2,1,0:T(8,128)(2,1)} %reshape.490), calls=%async_computation.7 | async-start | bytes 3276800 | tf_op jit(solution)/shard_map/all_to_all | solution.py:578
  494.2 20.6 %all-to-all-done.5 = bf16[8,12,6400]{2,1,0:T(8,128)(2,1)S(1)} async-done(((bf16[8,12,6400]{2,1,0:T(8,128)(2,1)}), bf16[8,12,6400]{2,1,0:T(8,128)(2,1)S(1)}, u32[]{:S(2)}, u32[]{:S(2)}) %all-to-all-start.5) | async-done | bytes 1228832 | tf_op jit(solution)/shard_map/all_to_all | solution.py:578
  (503 shorter events, 229.7 us)
Async XLA Ops:
  7.2 96.5 %all-gather.5.cloned.1.call-start = ((), (), s32[]{:S(2)}) async-start(), calls=%async_computation.8 | async-start | bytes 6266880 | tf_op jit(solution)/shard_map/all_gather | solution.py:624
  28.1 139.8 %all-gather.7.cloned.1.call-start = ((), (), s32[]{:S(2)}) async-start(), calls=%async_computation.9 | async-start | bytes 10027008 | tf_op jit(solution)/shard_map/all_gather | solution.py:635
  64.2 171.6 %all-gather.9.cloned.1.call-start = ((), (), s32[]{:S(2)}) async-start(), calls=%async_computation.12 | async-start | bytes 8355840 | tf_op jit(solution)/shard_map/all_gather | solution.py:688
  66.2 10.5 %collective-permute-start = (bf16[128,1536]{1,0:T(8,128)(2,1)S(1)}, bf16[128,1536]{1,0:T(8,128)(2,1)S(1)}, u32[]{:S(2)}, u32[]{:S(2)}) collective-permute-start(bf16[128,1536]{1,0:T(8,128)(2,1)S(1)} %bitcast.242), channel_id=1, source_target_pairs={{0,1},{1,0},{2,3},{3,2},{4,5},{5,4},{6,7},{7,6},{8,9},{9,8},{10,11... | collective-permute-start | bytes 1179656 | tf_op jit(solution)/shard_map/ppermute | solution.py:40
  69.9 23.5 %collective-permute-start.9 = (bf16[256,1536]{1,0:T(8,128)(2,1)S(1)}, bf16[256,1536]{1,0:T(8,128)(2,1)S(1)}, u32[]{:S(2)}, u32[]{:S(2)}) collective-permute-start(bf16[256,1536]{1,0:T(8,128)(2,1)S(1)} %bitcast.266), channel_id=1, source_target_pairs={{0,1},{1,0},{2,3},{3,2},{4,5},{5,4},{6,7},{7,6},{8,9},{9,8},{10,11... | collective-permute-start | bytes 2359304 | tf_op jit(solution)/shard_map/ppermute | solution.py:40
  76.9 19.7 %collective-permute-start.1 = (bf16[256,1536]{1,0:T(8,128)(2,1)S(1)}, bf16[256,1536]{1,0:T(8,128)(2,1)S(1)}, u32[]{:S(2)}, u32[]{:S(2)}) collective-permute-start(bf16[256,1536]{1,0:T(8,128)(2,1)S(1)} %maximum_select_fusion.3), channel_id=1, source_target_pairs={{0,2},{2,0},{1,3},{3,1},{4,6},{6,4},{5,7},{7,5},{8,10},{10,8},{9,1... | collective-permute-start | bytes 2359304 | tf_op jit(solution)/shard_map/ppermute | solution.py:40
  114.2 12.6 %collective-permute-start.13 = (f32[2,512]{0,1:T(8,128)S(1)}, f32[2,512]{0,1:T(8,128)S(1)}, u32[]{:S(2)}, u32[]{:S(2)}) collective-permute-start(f32[2,512]{0,1:T(8,128)S(1)} %bitcast.264), channel_id=1, source_target_pairs={{0,1},{1,0},{2,3},{3,2},{4,5},{5,4},{6,7},{7,6},{8,9},{9,8},{10,11... | collective-permute-start | bytes 12296 | tf_op jit(solution)/shard_map/ppermute | solution.py:40
  157.5 209.9 %reduce-scatter.3.cloned.1.call-start = ((), (), s32[]{:S(2)}) async-start(), calls=%async_computation.10 | async-start | bytes 8355840 | tf_op jit(solution)/shard_map/reduce_scatter | solution.py:746
  164.4 30.6 %collective-permute-start.26 = (bf16[256,768]{1,0:T(8,128)(2,1)S(1)}, bf16[256,768]{1,0:T(8,128)(2,1)S(1)}, u32[]{:S(2)}, u32[]{:S(2)}) collective-permute-start(bf16[256,768]{1,0:T(8,128)(2,1)S(1)} %fusion.34), channel_id=1, source_target_pairs={{0,5},{1,4},{4,1},{5,0},{2,7},{3,6},{6,3},{7,2},{8,13},{9,12},{12,... | collective-permute-start | bytes 1179656 | tf_op jit(solution)/shard_map/ppermute | solution.py:46
  165.4 29.7 %collective-permute-start.25 = (bf16[256,768]{1,0:T(8,128)(2,1)S(1)}, bf16[256,768]{1,0:T(8,128)(2,1)}, u32[]{:S(2)}, u32[]{:S(2)}) collective-permute-start(bf16[256,768]{1,0:T(8,128)(2,1)S(1)} %fusion.34), channel_id=1, source_target_pairs={{0,4},{1,5},{4,0},{5,1},{2,6},{3,7},{6,2},{7,3},{8,12},{9,13},{12,... | collective-permute-start | bytes 1179656 | tf_op jit(solution)/shard_map/ppermute | solution.py:46
  166.6 28.5 %collective-permute-start.24 = (bf16[256,768]{1,0:T(8,128)(2,1)S(1)}, bf16[256,768]{1,0:T(8,128)(2,1)}, u32[]{:S(2)}, u32[]{:S(2)}) collective-permute-start(bf16[256,768]{1,0:T(8,128)(2,1)S(1)} %fusion.34), channel_id=1, source_target_pairs={{0,1},{1,0},{4,5},{5,4},{2,3},{3,2},{6,7},{7,6},{8,9},{9,8},{12,13... | collective-permute-start | bytes 1179656 | tf_op jit(solution)/shard_map/ppermute | solution.py:46
  171.4 11.2 %collective-permute-start.22 = (f32[1,256]{1,0:T(1,128)S(1)}, f32[1,256]{1,0:T(1,128)S(1)}, u32[]{:S(2)}, u32[]{:S(2)}) collective-permute-start(f32[1,256]{1,0:T(1,128)S(1)} %bitcast.327), channel_id=1, source_target_pairs={{0,2},{2,0},{1,3},{3,1},{4,6},{6,4},{5,7},{7,5},{8,10},{10,8},{9,1... | collective-permute-start | bytes 3080 | tf_op jit(solution)/shard_map/ppermute | solution.py:40
  203.0 20.4 %collective-permute-start.31 = (bf16[256,768]{1,0:T(8,128)(2,1)S(1)}, bf16[256,768]{1,0:T(8,128)(2,1)S(1)}, u32[]{:S(2)}, u32[]{:S(2)}) collective-permute-start(bf16[256,768]{1,0:T(8,128)(2,1)S(1)} %fusion.38), channel_id=1, source_target_pairs={{0,5},{1,4},{4,1},{5,0},{2,7},{3,6},{6,3},{7,2},{8,13},{9,12},{12,... | collective-permute-start | bytes 1179656 | tf_op jit(solution)/shard_map/ppermute | solution.py:46
  204.0 19.4 %collective-permute-start.30 = (bf16[256,768]{1,0:T(8,128)(2,1)S(1)}, bf16[256,768]{1,0:T(8,128)(2,1)S(1)}, u32[]{:S(2)}, u32[]{:S(2)}) collective-permute-start(bf16[256,768]{1,0:T(8,128)(2,1)S(1)} %fusion.38), channel_id=1, source_target_pairs={{0,4},{1,5},{4,0},{5,1},{2,6},{3,7},{6,2},{7,3},{8,12},{9,13},{12,... | collective-permute-start | bytes 1179656 | tf_op jit(solution)/shard_map/ppermute | solution.py:46
  205.2 18.5 %collective-permute-start.29 = (bf16[256,768]{1,0:T(8,128)(2,1)S(1)}, bf16[256,768]{1,0:T(8,128)(2,1)S(1)}, u32[]{:S(2)}, u32[]{:S(2)}) collective-permute-start(bf16[256,768]{1,0:T(8,128)(2,1)S(1)} %fusion.38), channel_id=1, source_target_pairs={{0,1},{1,0},{4,5},{5,4},{2,3},{3,2},{6,7},{7,6},{8,9},{9,8},{12,13... | collective-permute-start | bytes 1179656 | tf_op jit(solution)/shard_map/ppermute | solution.py:46
  208.5 17.9 %collective-permute-start.33 = (bf16[1024,768]{1,0:T(8,128)(2,1)S(1)}, bf16[1024,768]{1,0:T(8,128)(2,1)S(1)}, u32[]{:S(2)}, u32[]{:S(2)}) collective-permute-start(bf16[1024,768]{1,0:T(8,128)(2,1)S(1)} %constant_dynamic-update-slice_fusion.g_ref), channel_id=1, source_target_pairs={{0,2},{2,0},{1,3},{3,1},{4,6},{6,4},{5,7},{7,5},{8,10},{10,8},{9,1... | collective-permute-start | bytes 4718600 | tf_op jit(solution)/shard_map/ppermute | solution.py:40
  262.7 18.6 %collective-permute-start.35 = (bf16[256,768]{1,0:T(8,128)(2,1)S(1)}, bf16[256,768]{1,0:T(8,128)(2,1)S(1)}, u32[]{:S(2)}, u32[]{:S(2)}) collective-permute-start(bf16[256,768]{1,0:T(8,128)(2,1)S(1)} %get-tuple-element.109), channel_id=1, source_target_pairs={{0,1},{1,0},{4,5},{5,4},{2,3},{3,2},{6,7},{7,6},{8,9},{9,8},{12,13... | collective-permute-start | bytes 1179656 | tf_op jit(solution)/shard_map/ppermute | solution.py:725
  264.1 19.9 %collective-permute-start.36 = (bf16[256,768]{1,0:T(8,128)(2,1)S(1)}, bf16[256,768]{1,0:T(8,128)(2,1)S(1)}, u32[]{:S(2)}, u32[]{:S(2)}) collective-permute-start(bf16[256,768]{1,0:T(8,128)(2,1)S(1)} %get-tuple-element.110), channel_id=1, source_target_pairs={{0,4},{1,5},{4,0},{5,1},{2,6},{3,7},{6,2},{7,3},{8,12},{9,13},{12,... | collective-permute-start | bytes 1179656 | tf_op jit(solution)/shard_map/ppermute | solution.py:725
  266.6 19.8 %collective-permute-start.37 = (bf16[256,768]{1,0:T(8,128)(2,1)S(1)}, bf16[256,768]{1,0:T(8,128)(2,1)}, u32[]{:S(2)}, u32[]{:S(2)}) collective-permute-start(bf16[256,768]{1,0:T(8,128)(2,1)S(1)} %get-tuple-element.111), channel_id=1, source_target_pairs={{0,5},{1,4},{4,1},{5,0},{2,7},{3,6},{6,3},{7,2},{8,13},{9,12},{12,... | collective-permute-start | bytes 1179656 | tf_op jit(solution)/shard_map/ppermute | solution.py:725
  286.5 195.2 %reduce-scatter.5.cloned.1.call-start = ((), (), s32[]{:S(2)}) async-start(), calls=%async_computation.11 | async-start | bytes 12533760 | tf_op jit(solution)/shard_map/reduce_scatter | solution.py:793
  308.1 22.3 %collective-permute-start.41 = (bf16[256,768]{1,0:T(8,128)(2,1)}, bf16[256,768]{1,0:T(8,128)(2,1)S(1)}, u32[]{:S(2)}, u32[]{:S(2)}) collective-permute-start(bf16[256,768]{1,0:T(8,128)(2,1)} %get-tuple-element.119), channel_id=1, source_target_pairs={{0,1},{1,0},{4,5},{5,4},{2,3},{3,2},{6,7},{7,6},{8,9},{9,8},{12,13... | collective-permute-start | bytes 1179656 | tf_op jit(solution)/shard_map/ppermute | solution.py:725
  308.3 22.1 %collective-permute-start.42 = (bf16[256,768]{1,0:T(8,128)(2,1)}, bf16[256,768]{1,0:T(8,128)(2,1)}, u32[]{:S(2)}, u32[]{:S(2)}) collective-permute-start(bf16[256,768]{1,0:T(8,128)(2,1)} %get-tuple-element.120), channel_id=1, source_target_pairs={{0,4},{1,5},{4,0},{5,1},{2,6},{3,7},{6,2},{7,3},{8,12},{9,13},{12,... | collective-permute-start | bytes 1179656 | tf_op jit(solution)/shard_map/ppermute | solution.py:725
  309.6 20.8 %collective-permute-start.43 = (bf16[256,768]{1,0:T(8,128)(2,1)}, bf16[256,768]{1,0:T(8,128)(2,1)}, u32[]{:S(2)}, u32[]{:S(2)}) collective-permute-start(bf16[256,768]{1,0:T(8,128)(2,1)} %get-tuple-element.121), channel_id=1, source_target_pairs={{0,5},{1,4},{4,1},{5,0},{2,7},{3,6},{6,3},{7,2},{8,13},{9,12},{12,... | collective-permute-start | bytes 1179656 | tf_op jit(solution)/shard_map/ppermute | solution.py:725
  394.6 12.5 %collective-permute-start.52 = (f32[2,512]{0,1:T(8,128)}, f32[2,512]{0,1:T(8,128)}, u32[]{:S(2)}, u32[]{:S(2)}) collective-permute-start(f32[2,512]{0,1:T(8,128)} %bitcast.277), channel_id=1, source_target_pairs={{0,1},{1,0},{2,3},{3,2},{4,5},{5,4},{6,7},{7,6},{8,9},{9,8},{10,11... | collective-permute-start | bytes 12296 | tf_op jit(solution)/shard_map/ppermute | solution.py:40
  426.0 34.7 %all-to-all-start.3 = ((bf16[4,384,640]{2,1,0:T(8,128)(2,1)}), bf16[4,384,640]{2,1,0:T(8,128)(2,1)S(1)}, u32[]{:S(2)}, u32[]{:S(2)}) async-start(bf16[4,384,640]{2,1,0:T(8,128)(2,1)} %bitcast.258), calls=%async_computation.5 | async-start | bytes 3932160 | tf_op jit(solution)/shard_map/all_to_all | solution.py:831
  433.3 39.4 %collective-permute-start.49 = (f32[128,768]{1,0:T(8,128)}, f32[128,768]{1,0:T(8,128)}, u32[]{:S(2)}, u32[]{:S(2)}) collective-permute-start(f32[128,768]{1,0:T(8,128)} %get-tuple-element.334), channel_id=1, source_target_pairs={{0,2},{2,0},{1,3},{3,1},{4,6},{6,4},{5,7},{7,5},{8,10},{10,8},{9,1... | collective-permute-start | bytes 1179656 | tf_op jit(solution)/shard_map/ppermute | solution.py:40
  434.2 24.9 %collective-permute-start.59 = (bf16[384,640]{1,0:T(8,128)(2,1)S(1)}, bf16[384,640]{1,0:T(8,128)(2,1)S(1)}, u32[]{:S(2)}, u32[]{:S(2)}) collective-permute-start(bf16[384,640]{1,0:T(8,128)(2,1)S(1)} %get-tuple-element.320), channel_id=1, source_target_pairs={{0,96},{32,64},{64,32},{96,0},{1,97},{33,65},{65,33},{97,1},{2,98}... | collective-permute-start | bytes 1474568 | tf_op jit(solution)/shard_map/ppermute | solution.py:833
  436.4 22.8 %collective-permute-start.58 = (bf16[384,640]{1,0:T(8,128)(2,1)S(1)}, bf16[384,640]{1,0:T(8,128)(2,1)S(1)}, u32[]{:S(2)}, u32[]{:S(2)}) collective-permute-start(bf16[384,640]{1,0:T(8,128)(2,1)S(1)} %get-tuple-element.321), channel_id=1, source_target_pairs={{0,64},{32,96},{64,0},{96,32},{1,65},{33,97},{65,1},{97,33},{2,66}... | collective-permute-start | bytes 1474568 | tf_op jit(solution)/shard_map/ppermute | solution.py:833
  437.0 23.7 %collective-permute-start.57 = (bf16[384,640]{1,0:T(8,128)(2,1)S(1)}, bf16[384,640]{1,0:T(8,128)(2,1)}, u32[]{:S(2)}, u32[]{:S(2)}) collective-permute-start(bf16[384,640]{1,0:T(8,128)(2,1)S(1)} %get-tuple-element.322), channel_id=1, source_target_pairs={{0,32},{32,0},{64,96},{96,64},{1,33},{33,1},{65,97},{97,65},{2,34}... | collective-permute-start | bytes 1474568 | tf_op jit(solution)/shard_map/ppermute | solution.py:833
  464.5 16.1 %all-to-all-start.4 = ((bf16[4,96,640]{2,1,0:T(8,128)(2,1)}), bf16[4,96,640]{2,1,0:T(8,128)(2,1)S(1)}, u32[]{:S(2)}, u32[]{:S(2)}) async-start(bf16[4,96,640]{2,1,0:T(8,128)(2,1)} %bitcast.90), calls=%async_computation.6 | async-start | bytes 983040 | tf_op jit(solution)/shard_map/all_to_all | solution.py:831
  469.3 10.6 %collective-permute-start.62 = (bf16[96,640]{1,0:T(8,128)(2,1)S(1)}, bf16[96,640]{1,0:T(8,128)(2,1)S(1)}, u32[]{:S(2)}, u32[]{:S(2)}) collective-permute-start(bf16[96,640]{1,0:T(8,128)(2,1)S(1)} %get-tuple-element.345), channel_id=1, source_target_pairs={{0,96},{32,64},{64,32},{96,0},{1,97},{33,65},{65,33},{97,1},{2,98}... | collective-permute-start | bytes 368648 | tf_op jit(solution)/shard_map/ppermute | solution.py:833
  487.8 27.0 %all-to-all-start.5 = ((bf16[8,12,6400]{2,1,0:T(8,128)(2,1)}), bf16[8,12,6400]{2,1,0:T(8,128)(2,1)S(1)}, u32[]{:S(2)}, u32[]{:S(2)}) async-start(bf16[8,12,6400]{2,1,0:T(8,128)(2,1)} %reshape.490), calls=%async_computation.7 | async-start | bytes 3276800 | tf_op jit(solution)/shard_map/all_to_all | solution.py:578
  (99 other events, 960.5 us)
Sparse Core Ops, SparseCore 0:
  28.2 59.3 all-gather.4
  89.7 75.1 all-gather.6
  167.6 68.1 all-gather.8
  286.6 80.7 reduce-scatter.2
  371.1 106.9 reduce-scatter.4

commit v3 on v2

--- a/solution.py
+++ b/solution.py
@@ -725,8 +725,10 @@
         return [lax.ppermute(blocks[k], CHIPS, [(i, i ^ (k + 1)) for i in range(4)]) for k in range(3)]
 
     def core_lines(keep, give):
-        lines = keep.astype(f32) + swap(give, "core").astype(f32)
-        return lines[: 2 * tokens], jnp.split(lines[2 * tokens :].astype(bf16), 3, 0)
+        got = swap(give, "core")
+        near = keep[: 2 * tokens].astype(f32) + got[: 2 * tokens].astype(f32)
+        far = keep[2 * tokens :].astype(f32) + got[2 * tokens :].astype(f32)
+        return near, jnp.split(far.astype(bf16), 3, 0)
 
     near_input, far = core_lines(keep, give)
     down_weight = jnp.concatenate(

time: 542 us -> 540 us (level)
  waiting for transfers between devices: 146 us -> 135 us
    unnamed x158 -> x154, local copies, waits for them, and re-layouts: 18.7 us -> 20.2 us
  transfers between devices with their start and end apart: 71 -> 71, of which waited for: 34 -> 36; matrix products, arithmetic and copies ran while one was open for 21% -> 23% of each run, Pallas kernels for 15% -> 15%
where the time goes in v3:
time: 540 us; the launch traced here: 531 us
  waiting for transfers between devices  135 us (25%)
  Pallas kernels  100 us (19%)
  starting transfers between devices  79.6 us (15%)
  other arithmetic  70.9 us (13%)
  local copies, waits for them, and re-layouts  49.1 us (9%)
  blocking collectives  45.2 us (8%)
  matrix products  34.6 us (6%)
  between operations  16.2 us (3%)
    ppermute x37, waiting for transfers between devices, swap(): return lax.ppermute(array, axis_name, SWAP)  52.7 us
    all_to_all x3, blocking collectives, along_line(): return lax.all_to_all(parts, LINE, split_axis=0, concat_axis=0, tiled=True)  45.2 us
    ppermute x37, starting transfers between devices, swap(): return lax.ppermute(array, axis_name, SWAP)  32.6 us
    dot_general x6, matrix products, mm(): return jnp.dot(left, right, preferred_element_type=f32)  26.8 us
    ppermute x12, waiting for transfers between devices, others(): lax.ppermute(array, axis_name, [(i, i ^ k) for i in range(size)])  20.3 us
    pallas_call x4, Pallas kernels, tn_pack(): pl.pallas_call(functools.partial(tn_pack_kernel, place), in_specs=[vmem,...  20.3 us
    unnamed x154, local copies, waits for them, and re-layouts  20.2 us
    ppermute x6, waiting for transfers between devices, sum_both(): lax.ppermute(by_y[k], 'y', [(at, at ^ k) for at in range(down_across[0])])  19.6 us
  transfers between devices with their start and end apart: 71, of which 36 were waited for; matrix products, arithmetic and copies ran while one was open for 23% of the time, Pallas kernels for 15%

profile of v3, /device:TPU:1, one launch (start us, length us, event | category | flops | bytes accessed | tf_op | source)
XLA Modules:
  0.0 530.5 jit_solution(15560595948903428316)
XLA Ops:
  11.4 15.8 %all_to_all.30 = bf16[8,12,2048]{2,1,0:T(8,128)(2,1)S(1)} all-to-all(bf16[8,12,2048]{2,1,0:T(8,128)(2,1)S(1)} %copy.187), channel_id=1, replica_groups=mesh['y'=4,'x'=4,'zh'=2,'core'=2,'zl'=2] {'zh','core','zl'}, dimensions={0} | all-to-all | bytes 786432 | tf_op jit(solution)/shard_map/all_to_all | solution.py:578
  44.5 18.7 %all_to_all.31 = bf16[8,12,3072]{2,1,0:T(8,128)(2,1)S(1)} all-to-all(bf16[8,12,3072]{2,1,0:T(8,128)(2,1)S(1)} %pad_maximum_fusion.3), channel_id=1, replica_groups=mesh['y'=4,'x'=4,'zh'=2,'core'=2,'zl'=2] {'zh','core','zl'}, dimensions={0} | all-to-all | bytes 1179648 | tf_op jit(solution)/shard_map/all_to_all | solution.py:578
  79.0 14.5 %collective-permute-done.9 = bf16[256,1536]{1,0:T(8,128)(2,1)S(1)} collective-permute-done((bf16[256,1536]{1,0:T(8,128)(2,1)}, bf16[256,1536]{1,0:T(8,128)(2,1)S(1)}, u32[]{:S(2)}, u32[]{:S(2)}) %collective-permute-start.9) | collective-permute-done | bytes 786464 | tf_op jit(solution)/shard_map/ppermute | solution.py:40
  98.9 3.9 fusion.4
  105.0 6.5 %fusion.89 = (f32[512,1152]{1,0:T(8,128)}, f32[512,1152]{1,0:T(8,128)}) fusion(bf16[512,1536]{1,0:T(8,128)(2,1)S(1)} %copy-done.28, bf16[1536,1920]{1,0:T(8,128)(2,1)} %all-gather.5.cloned.1.call-done.w_ref), kind=kOutput, calls=%fused_computation.338 | convolution fusion | flops 1812529152 | bytes 9830400 | tf_op jit(solution)/shard_map/dot_general | solution.py:28
  118.9 6.2 %collective-permute-done.15 = f32[2,512]{0,1:T(8,128)S(1)} collective-permute-done((f32[2,512]{0,1:T(8,128)S(1)}, f32[2,512]{0,1:T(8,128)S(1)}, u32[]{:S(2)}, u32[]{:S(2)}) %collective-permute-start.15) | collective-permute-done | bytes 4128 | tf_op jit(solution)/shard_map/ppermute | solution.py:69
  125.1 5.5 %collective-permute-done.13 = f32[2,512]{0,1:T(8,128)S(1)} collective-permute-done((f32[2,512]{0,1:T(8,128)S(1)}, f32[2,512]{0,1:T(8,128)S(1)}, u32[]{:S(2)}, u32[]{:S(2)}) %collective-permute-start.13) | collective-permute-done | bytes 4128 | tf_op jit(solution)/shard_map/ppermute | solution.py:40
  131.4 7.4 %self_forward.1 = (bf16[512,384]{1,0:T(8,128)(2,1)}, bf16[512,384]{1,0:T(8,128)(2,1)}, bf16[512,384]{1,0:T(8,128)(2,1)}, bf16[512,384]{1,0:T(8,128)(2,1)}) custom-call(f32[512,1152]{1,0:T(8,128)} %get-tuple-element.393.q_ref.k_ref.v_ref, f32[512,1152]{1,0:T(8,128)} %get-tuple-element.393.q_ref.k_ref.v_ref, f32[512,1152]{1,0:T(8,128)} %get-tuple-element.393.q_ref.k_ref.v_ref, ...), custom_call_target="tpu_custom_call" | custom-call | flops 8000000000 | bytes 10000000 | tf_op jit(solution)/shard_map/self_forward/pallas_call | solution.py:182
  141.1 4.8 collective-permute-done.18
  149.5 10.7 %all_to_all.32 = bf16[8,12,1280]{2,1,0:T(8,128)(2,1)S(1)} all-to-all(bf16[8,12,1280]{2,1,0:T(8,128)(2,1)S(1)} %copy.196), channel_id=1, replica_groups=mesh['y'=4,'x'=4,'zh'=2,'core'=2,'zl'=2] {'zh','core','zl'}, dimensions={0} | all-to-all | bytes 491520 | tf_op jit(solution)/shard_map/all_to_all | solution.py:578
  176.4 7.1 %fusion = f32[1024,1536]{1,0:T(8,128)S(1)} fusion(bf16[1024,1536]{1,0:T(8,128)(2,1)S(1)} %copy-done.2, bf16[1536,3072]{1,0:T(8,128)(2,1)} %all-gather.7.cloned.1.call-done), kind=kOutput, calls=%fused_computation | convolution fusion | flops 4831838208 | bytes 14155776 | tf_op jit(solution)/shard_map/dot_general | solution.py:28
  191.2 7.8 %cross_forward.1 = (bf16[256,768]{1,0:T(8,128)(2,1)}, bf16[256,768]{1,0:T(8,128)(2,1)}) custom-call(f32[256,768]{1,0:T(8,128)} %get-tuple-element.395.q_ref, f32[256,1]{1,0:T(8,128)} %copy.195.r_ref, f32[1,768]{1,0:T(1,128)} %get-tuple-element.300.g_ref, bf16[1024,768]{1,0:T(8,128)(2,1)} %multiply_convert_fusion.1.k_ref, bf16[1024,768]{1,0:T(8,128)(2,1)} %slice.626.v_ref), custom_call_target="tpu_custom_call" | custom-call | flops 8999999488 | bytes 10000000 | tf_op jit(solution)/shard_map/cross_forward/pallas_call | solution.py:263
  214.7 12.8 %collective-permute-done.31 = bf16[256,768]{1,0:T(8,128)(2,1)S(1)} collective-permute-done((bf16[256,768]{1,0:T(8,128)(2,1)S(1)}, bf16[256,768]{1,0:T(8,128)(2,1)S(1)}, u32[]{:S(2)}, u32[]{:S(2)}) %collective-permute-start.31) | collective-permute-done | bytes 393248 | tf_op jit(solution)/shard_map/ppermute | solution.py:46
  235.9 19.3 %mlp.1 = (bf16[1024,1280]{1,0:T(8,128)(2,1)}, bf16[1024,1280]{1,0:T(8,128)(2,1)}, bf16[1024,768]{1,0:T(8,128)(2,1)}, bf16[1024,768]{1,0:T(8,128)(2,1)}) custom-call(s32[1]{0:T(128)} %bitcast.47.core_ref, bf16[1024,768]{1,0:T(8,128)(2,1)} %copy-done.25, bf16[1024,768]{1,0:T(8,128)(2,1)} %collective-permute-done.32.xo_ref, bf16[1024,768]{1,0:T(8,128)(2,1)} %copy-done.49, ...), custom_call_target="tpu_custom_call" | custom-call | flops 12079595520 | bytes 7864320 | tf_op jit(solution)/shard_map/mlp/pallas_call | solution.py:374
  265.9 14.3 %mlp_grads.1 = bf16[16,960,256]{2,1,0:T(8,128)(2,1)} custom-call(s32[1]{0:T(128)} %bitcast.47.core_ref, bf16[1024,768]{1,0:T(8,128)(2,1)} %copy-done.25, bf16[1024,768]{1,0:T(8,128)(2,1)} %collective-permute-done.32.xo_ref, bf16[1024,1280]{1,0:T(8,128)(2,1)} %get-tuple-element.107.gh_ref, bf16[1024,1280]{1,0:T(8,128)(2,1)} %get-tuple-element.108.act_ref, ...), custom_call_target="tpu_custom_call" | custom-call | flops 8053063680 | bytes 7864320 | tf_op jit(solution)/shard_map/mlp_grads/pallas_call | solution.py:476
  289.6 4.4 convolution_convert_fusion
  310.9 9.8 %cross_backward.1 = (f32[256,768]{1,0:T(8,128)}, f32[1024,768]{1,0:T(8,128)}, bf16[1024,768]{1,0:T(8,128)(2,1)}) custom-call(bf16[256,768]{1,0:T(8,128)(2,1)} %get-tuple-element.116.qn_ref, bf16[1024,768]{1,0:T(8,128)(2,1)} %multiply_convert_fusion.1.k_ref, bf16[1024,768]{1,0:T(8,128)(2,1)} %slice.626.v_ref, bf16[256,768]{1,0:T(8,128)(2,1)} %add_convert_fusion.4.do_ref), custom_call_target="tpu_custom_call" | custom-call | flops 11000000512 | bytes 10000000 | tf_op jit(solution)/shard_map/cross_backward/pallas_call | solution.py:291
  320.8 3.8 multiply_reduce_fusion
  325.7 3.6 tn_pack.4.rest_0_
  341.1 3.6 tn_pack.5.rest_0_
  346.9 9.5 %tn_pack.6.rest_0_ = bf16[16,480,768]{2,1,0:T(8,128)(2,1)} custom-call(bf16[1024,1536]{1,0:T(8,128)(2,1)} %maximum_select_fusion.x_ref, bf16[1024,1536]{1,0:T(8,128)(2,1)} %pad_maximum_fusion.g_ref, bf16[16,480,768]{2,1,0:T(8,128)(2,1)} %tn_pack.5.rest_0_), custom_call_target="tpu_custom_call", output_to_operand_aliasing={{}: (2, {})} | custom-call | flops 4831838208 | bytes 4718592 | tf_op jit(solution)/shard_map/tn_pack/pallas_call | solution.py:427
  359.6 3.6 tn_pack.7
  380.4 10.3 %self_backward.1 = (f32[512,384]{1,0:T(8,128)}, f32[512,384]{1,0:T(8,128)}, bf16[512,384]{1,0:T(8,128)(2,1)}, f32[512,2]{1,0:T(8,128)}, f32[2,3,2,128]{3,2,1,0:T(2,128)}) custom-call(bf16[512,384]{1,0:T(8,128)(2,1)} %get-tuple-element.130.qr_ref, bf16[512,384]{1,0:T(8,128)(2,1)} %get-tuple-element.131.kr_ref, bf16[512,384]{1,0:T(8,128)(2,1)} %get-tuple-element.132.vb_ref, ...), custom_call_target="tpu_custom_call" | custom-call | flops 11000000512 | bytes 10000000 | tf_op jit(solution)/shard_map/self_backward/pallas_call | solution.py:232
  395.7 5.4 %collective-permute-done.54 = f32[2,512]{0,1:T(8,128)} collective-permute-done((f32[2,512]{0,1:T(8,128)}, f32[2,512]{0,1:T(8,128)}, u32[]{:S(2)}, u32[]{:S(2)}) %collective-permute-start.54) | collective-permute-done | bytes 4128 | tf_op jit(solution)/shard_map/ppermute | solution.py:69
  401.1 4.5 collective-permute-done.52
  409.0 11.1 %tail.1 = (bf16[1536,640]{1,0:T(8,128)(2,1)}, bf16[1536,640]{1,0:T(8,128)(2,1)}, bf16[256,1536]{1,0:T(8,128)(2,1)}, bf16[256,1536]{1,0:T(8,128)(2,1)}) custom-call(s32[2]{0:T(128)} %pad_add_fusion.at_ref, bf16[512,1536]{1,0:T(8,128)(2,1)} %get-tuple-element.88.x_ref, bf16[512,1152]{1,0:T(8,128)(2,1)} %pad_maximum_fusion.2.g_ref, ...), custom_call_target="tpu_custom_call" | custom-call | flops 8000000000 | bytes 10000000 | tf_op jit(solution)/shard_map/tail/pallas_call | solution.py:538
  424.5 3.6 all-to-all-start.3
  436.5 3.9 collective-permute-done.56
  440.7 17.1 %collective-permute-done.59 = bf16[384,640]{1,0:T(8,128)(2,1)S(1)} collective-permute-done((bf16[384,640]{1,0:T(8,128)(2,1)S(1)}, bf16[384,640]{1,0:T(8,128)(2,1)S(1)}, u32[]{:S(2)}, u32[]{:S(2)}) %collective-permute-start.59) | collective-permute-done | bytes 491552 | tf_op jit(solution)/shard_map/ppermute | solution.py:835
  463.2 4.7 all-to-all-start.4
  485.1 6.0 %all-to-all-start.5 = ((bf16[8,12,6400]{2,1,0:T(8,128)(2,1)}), bf16[8,12,6400]{2,1,0:T(8,128)(2,1)S(1)}, u32[]{:S(2)}, u32[]{:S(2)}) async-start(bf16[8,12,6400]{2,1,0:T(8,128)(2,1)} %reshape.490), calls=%async_computation.7 | async-start | bytes 3276800 | tf_op jit(solution)/shard_map/all_to_all | solution.py:578
  494.2 18.3 %all-to-all-done.5 = bf16[8,12,6400]{2,1,0:T(8,128)(2,1)S(1)} async-done(((bf16[8,12,6400]{2,1,0:T(8,128)(2,1)}), bf16[8,12,6400]{2,1,0:T(8,128)(2,1)S(1)}, u32[]{:S(2)}, u32[]{:S(2)}) %all-to-all-start.5) | async-done | bytes 1228832 | tf_op jit(solution)/shard_map/all_to_all | solution.py:578
  (499 shorter events, 235.8 us)
Async XLA Ops:
  7.2 97.8 %all-gather.5.cloned.1.call-start = ((), (), s32[]{:S(2)}) async-start(), calls=%async_computation.8 | async-start | bytes 6266880 | tf_op jit(solution)/shard_map/all_gather | solution.py:624
  28.1 143.7 %all-gather.7.cloned.1.call-start = ((), (), s32[]{:S(2)}) async-start(), calls=%async_computation.9 | async-start | bytes 10027008 | tf_op jit(solution)/shard_map/all_gather | solution.py:635
  64.2 171.7 %all-gather.9.cloned.1.call-start = ((), (), s32[]{:S(2)}) async-start(), calls=%async_computation.12 | async-start | bytes 8355840 | tf_op jit(solution)/shard_map/all_gather | solution.py:688
  66.3 10.5 %collective-permute-start = (bf16[128,1536]{1,0:T(8,128)(2,1)S(1)}, bf16[128,1536]{1,0:T(8,128)(2,1)S(1)}, u32[]{:S(2)}, u32[]{:S(2)}) collective-permute-start(bf16[128,1536]{1,0:T(8,128)(2,1)S(1)} %bitcast.242), channel_id=1, source_target_pairs={{0,1},{1,0},{2,3},{3,2},{4,5},{5,4},{6,7},{7,6},{8,9},{9,8},{10,11... | collective-permute-start | bytes 1179656 | tf_op jit(solution)/shard_map/ppermute | solution.py:40
  70.0 23.5 %collective-permute-start.9 = (bf16[256,1536]{1,0:T(8,128)(2,1)}, bf16[256,1536]{1,0:T(8,128)(2,1)S(1)}, u32[]{:S(2)}, u32[]{:S(2)}) collective-permute-start(bf16[256,1536]{1,0:T(8,128)(2,1)} %bitcast.22), channel_id=1, source_target_pairs={{0,1},{1,0},{2,3},{3,2},{4,5},{5,4},{6,7},{7,6},{8,9},{9,8},{10,11... | collective-permute-start | bytes 2359304 | tf_op jit(solution)/shard_map/ppermute | solution.py:40
  76.9 20.8 %collective-permute-start.1 = (bf16[256,1536]{1,0:T(8,128)(2,1)S(1)}, bf16[256,1536]{1,0:T(8,128)(2,1)S(1)}, u32[]{:S(2)}, u32[]{:S(2)}) collective-permute-start(bf16[256,1536]{1,0:T(8,128)(2,1)S(1)} %maximum_select_fusion.3), channel_id=1, source_target_pairs={{0,2},{2,0},{1,3},{3,1},{4,6},{6,4},{5,7},{7,5},{8,10},{10,8},{9,1... | collective-permute-start | bytes 2359304 | tf_op jit(solution)/shard_map/ppermute | solution.py:40
  118.0 12.6 %collective-permute-start.13 = (f32[2,512]{0,1:T(8,128)S(1)}, f32[2,512]{0,1:T(8,128)S(1)}, u32[]{:S(2)}, u32[]{:S(2)}) collective-permute-start(f32[2,512]{0,1:T(8,128)S(1)} %bitcast.264), channel_id=1, source_target_pairs={{0,1},{1,0},{2,3},{3,2},{4,5},{5,4},{6,7},{7,6},{8,9},{9,8},{10,11... | collective-permute-start | bytes 12296 | tf_op jit(solution)/shard_map/ppermute | solution.py:40
  161.3 204.7 %reduce-scatter.3.cloned.1.call-start = ((), (), s32[]{:S(2)}) async-start(), calls=%async_computation.10 | async-start | bytes 8355840 | tf_op jit(solution)/shard_map/reduce_scatter | solution.py:748
  168.3 30.8 %collective-permute-start.26 = (bf16[256,768]{1,0:T(8,128)(2,1)S(1)}, bf16[256,768]{1,0:T(8,128)(2,1)}, u32[]{:S(2)}, u32[]{:S(2)}) collective-permute-start(bf16[256,768]{1,0:T(8,128)(2,1)S(1)} %fusion.34), channel_id=1, source_target_pairs={{0,5},{1,4},{4,1},{5,0},{2,7},{3,6},{6,3},{7,2},{8,13},{9,12},{12,... | collective-permute-start | bytes 1179656 | tf_op jit(solution)/shard_map/ppermute | solution.py:46
  169.2 29.8 %collective-permute-start.25 = (bf16[256,768]{1,0:T(8,128)(2,1)S(1)}, bf16[256,768]{1,0:T(8,128)(2,1)}, u32[]{:S(2)}, u32[]{:S(2)}) collective-permute-start(bf16[256,768]{1,0:T(8,128)(2,1)S(1)} %fusion.34), channel_id=1, source_target_pairs={{0,4},{1,5},{4,0},{5,1},{2,6},{3,7},{6,2},{7,3},{8,12},{9,13},{12,... | collective-permute-start | bytes 1179656 | tf_op jit(solution)/shard_map/ppermute | solution.py:46
  170.4 28.6 %collective-permute-start.24 = (bf16[256,768]{1,0:T(8,128)(2,1)S(1)}, bf16[256,768]{1,0:T(8,128)(2,1)}, u32[]{:S(2)}, u32[]{:S(2)}) collective-permute-start(bf16[256,768]{1,0:T(8,128)(2,1)S(1)} %fusion.34), channel_id=1, source_target_pairs={{0,1},{1,0},{4,5},{5,4},{2,3},{3,2},{6,7},{7,6},{8,9},{9,8},{12,13... | collective-permute-start | bytes 1179656 | tf_op jit(solution)/shard_map/ppermute | solution.py:46
  175.2 11.3 %collective-permute-start.22 = (f32[1,256]{1,0:T(1,128)S(1)}, f32[1,256]{1,0:T(1,128)S(1)}, u32[]{:S(2)}, u32[]{:S(2)}) collective-permute-start(f32[1,256]{1,0:T(1,128)S(1)} %bitcast.325), channel_id=1, source_target_pairs={{0,2},{2,0},{1,3},{3,1},{4,6},{6,4},{5,7},{7,5},{8,10},{10,8},{9,1... | collective-permute-start | bytes 3080 | tf_op jit(solution)/shard_map/ppermute | solution.py:40
  207.2 20.4 %collective-permute-start.31 = (bf16[256,768]{1,0:T(8,128)(2,1)S(1)}, bf16[256,768]{1,0:T(8,128)(2,1)S(1)}, u32[]{:S(2)}, u32[]{:S(2)}) collective-permute-start(bf16[256,768]{1,0:T(8,128)(2,1)S(1)} %fusion.38), channel_id=1, source_target_pairs={{0,5},{1,4},{4,1},{5,0},{2,7},{3,6},{6,3},{7,2},{8,13},{9,12},{12,... | collective-permute-start | bytes 1179656 | tf_op jit(solution)/shard_map/ppermute | solution.py:46
  208.3 19.3 %collective-permute-start.30 = (bf16[256,768]{1,0:T(8,128)(2,1)S(1)}, bf16[256,768]{1,0:T(8,128)(2,1)S(1)}, u32[]{:S(2)}, u32[]{:S(2)}) collective-permute-start(bf16[256,768]{1,0:T(8,128)(2,1)S(1)} %fusion.38), channel_id=1, source_target_pairs={{0,4},{1,5},{4,0},{5,1},{2,6},{3,7},{6,2},{7,3},{8,12},{9,13},{12,... | collective-permute-start | bytes 1179656 | tf_op jit(solution)/shard_map/ppermute | solution.py:46
  209.0 18.8 %collective-permute-start.29 = (bf16[256,768]{1,0:T(8,128)(2,1)S(1)}, bf16[256,768]{1,0:T(8,128)(2,1)S(1)}, u32[]{:S(2)}, u32[]{:S(2)}) collective-permute-start(bf16[256,768]{1,0:T(8,128)(2,1)S(1)} %fusion.38), channel_id=1, source_target_pairs={{0,1},{1,0},{4,5},{5,4},{2,3},{3,2},{6,7},{7,6},{8,9},{9,8},{12,13... | collective-permute-start | bytes 1179656 | tf_op jit(solution)/shard_map/ppermute | solution.py:46
  213.7 16.8 %collective-permute-start.33 = (bf16[1024,768]{1,0:T(8,128)(2,1)S(1)}, bf16[1024,768]{1,0:T(8,128)(2,1)S(1)}, u32[]{:S(2)}, u32[]{:S(2)}) collective-permute-start(bf16[1024,768]{1,0:T(8,128)(2,1)S(1)} %constant_dynamic-update-slice_fusion.g_ref), channel_id=1, source_target_pairs={{0,2},{2,0},{1,3},{3,1},{4,6},{6,4},{5,7},{7,5},{8,10},{10,8},{9,1... | collective-permute-start | bytes 4718600 | tf_op jit(solution)/shard_map/ppermute | solution.py:40
  261.6 18.6 %collective-permute-start.35 = (bf16[256,768]{1,0:T(8,128)(2,1)S(1)}, bf16[256,768]{1,0:T(8,128)(2,1)S(1)}, u32[]{:S(2)}, u32[]{:S(2)}) collective-permute-start(bf16[256,768]{1,0:T(8,128)(2,1)S(1)} %get-tuple-element.109), channel_id=1, source_target_pairs={{0,1},{1,0},{4,5},{5,4},{2,3},{3,2},{6,7},{7,6},{8,9},{9,8},{12,13... | collective-permute-start | bytes 1179656 | tf_op jit(solution)/shard_map/ppermute | solution.py:725
  262.9 20.0 %collective-permute-start.36 = (bf16[256,768]{1,0:T(8,128)(2,1)S(1)}, bf16[256,768]{1,0:T(8,128)(2,1)}, u32[]{:S(2)}, u32[]{:S(2)}) collective-permute-start(bf16[256,768]{1,0:T(8,128)(2,1)S(1)} %get-tuple-element.110), channel_id=1, source_target_pairs={{0,4},{1,5},{4,0},{5,1},{2,6},{3,7},{6,2},{7,3},{8,12},{9,13},{12,... | collective-permute-start | bytes 1179656 | tf_op jit(solution)/shard_map/ppermute | solution.py:725
  265.5 19.8 %collective-permute-start.37 = (bf16[256,768]{1,0:T(8,128)(2,1)S(1)}, bf16[256,768]{1,0:T(8,128)(2,1)}, u32[]{:S(2)}, u32[]{:S(2)}) collective-permute-start(bf16[256,768]{1,0:T(8,128)(2,1)S(1)} %get-tuple-element.111), channel_id=1, source_target_pairs={{0,5},{1,4},{4,1},{5,0},{2,7},{3,6},{6,3},{7,2},{8,13},{9,12},{12,... | collective-permute-start | bytes 1179656 | tf_op jit(solution)/shard_map/ppermute | solution.py:725
  285.3 193.6 %reduce-scatter.5.cloned.1.call-start = ((), (), s32[]{:S(2)}) async-start(), calls=%async_computation.11 | async-start | bytes 12533760 | tf_op jit(solution)/shard_map/reduce_scatter | solution.py:795
  306.9 22.4 %collective-permute-start.41 = (bf16[256,768]{1,0:T(8,128)(2,1)}, bf16[256,768]{1,0:T(8,128)(2,1)}, u32[]{:S(2)}, u32[]{:S(2)}) collective-permute-start(bf16[256,768]{1,0:T(8,128)(2,1)} %get-tuple-element.119), channel_id=1, source_target_pairs={{0,1},{1,0},{4,5},{5,4},{2,3},{3,2},{6,7},{7,6},{8,9},{9,8},{12,13... | collective-permute-start | bytes 1179656 | tf_op jit(solution)/shard_map/ppermute | solution.py:725
  307.1 22.2 %collective-permute-start.42 = (bf16[256,768]{1,0:T(8,128)(2,1)}, bf16[256,768]{1,0:T(8,128)(2,1)}, u32[]{:S(2)}, u32[]{:S(2)}) collective-permute-start(bf16[256,768]{1,0:T(8,128)(2,1)} %get-tuple-element.120), channel_id=1, source_target_pairs={{0,4},{1,5},{4,0},{5,1},{2,6},{3,7},{6,2},{7,3},{8,12},{9,13},{12,... | collective-permute-start | bytes 1179656 | tf_op jit(solution)/shard_map/ppermute | solution.py:725
  308.5 20.9 %collective-permute-start.43 = (bf16[256,768]{1,0:T(8,128)(2,1)}, bf16[256,768]{1,0:T(8,128)(2,1)}, u32[]{:S(2)}, u32[]{:S(2)}) collective-permute-start(bf16[256,768]{1,0:T(8,128)(2,1)} %get-tuple-element.121), channel_id=1, source_target_pairs={{0,5},{1,4},{4,1},{5,0},{2,7},{3,6},{6,3},{7,2},{8,13},{9,12},{12,... | collective-permute-start | bytes 1179656 | tf_op jit(solution)/shard_map/ppermute | solution.py:725
  393.1 12.5 %collective-permute-start.52 = (f32[2,512]{0,1:T(8,128)}, f32[2,512]{0,1:T(8,128)}, u32[]{:S(2)}, u32[]{:S(2)}) collective-permute-start(f32[2,512]{0,1:T(8,128)} %bitcast.275), channel_id=1, source_target_pairs={{0,1},{1,0},{2,3},{3,2},{4,5},{5,4},{6,7},{7,6},{8,9},{9,8},{10,11... | collective-permute-start | bytes 12296 | tf_op jit(solution)/shard_map/ppermute | solution.py:40
  424.5 34.9 %all-to-all-start.3 = ((bf16[4,384,640]{2,1,0:T(8,128)(2,1)}), bf16[4,384,640]{2,1,0:T(8,128)(2,1)S(1)}, u32[]{:S(2)}, u32[]{:S(2)}) async-start(bf16[4,384,640]{2,1,0:T(8,128)(2,1)} %bitcast.258), calls=%async_computation.5 | async-start | bytes 3932160 | tf_op jit(solution)/shard_map/all_to_all | solution.py:833
  430.0 10.4 %collective-permute-start.56 = (bf16[128,1536]{1,0:T(8,128)(2,1)S(1)}, bf16[128,1536]{1,0:T(8,128)(2,1)S(1)}, u32[]{:S(2)}, u32[]{:S(2)}) collective-permute-start(bf16[128,1536]{1,0:T(8,128)(2,1)S(1)} %select_convert_fusion), channel_id=1, source_target_pairs={{0,1},{1,0},{2,3},{3,2},{4,5},{5,4},{6,7},{7,6},{8,9},{9,8},{10,11... | collective-permute-start | bytes 1179656 | tf_op jit(solution)/shard_map/ppermute | solution.py:40
  432.2 39.1 %collective-permute-start.49 = (f32[128,768]{1,0:T(8,128)}, f32[128,768]{1,0:T(8,128)}, u32[]{:S(2)}, u32[]{:S(2)}) collective-permute-start(f32[128,768]{1,0:T(8,128)} %get-tuple-element.332), channel_id=1, source_target_pairs={{0,2},{2,0},{1,3},{3,1},{4,6},{6,4},{5,7},{7,5},{8,10},{10,8},{9,1... | collective-permute-start | bytes 1179656 | tf_op jit(solution)/shard_map/ppermute | solution.py:40
  433.2 24.7 %collective-permute-start.59 = (bf16[384,640]{1,0:T(8,128)(2,1)S(1)}, bf16[384,640]{1,0:T(8,128)(2,1)S(1)}, u32[]{:S(2)}, u32[]{:S(2)}) collective-permute-start(bf16[384,640]{1,0:T(8,128)(2,1)S(1)} %get-tuple-element.318), channel_id=1, source_target_pairs={{0,96},{32,64},{64,32},{96,0},{1,97},{33,65},{65,33},{97,1},{2,98}... | collective-permute-start | bytes 1474568 | tf_op jit(solution)/shard_map/ppermute | solution.py:835
  435.3 22.6 %collective-permute-start.58 = (bf16[384,640]{1,0:T(8,128)(2,1)S(1)}, bf16[384,640]{1,0:T(8,128)(2,1)S(1)}, u32[]{:S(2)}, u32[]{:S(2)}) collective-permute-start(bf16[384,640]{1,0:T(8,128)(2,1)S(1)} %get-tuple-element.319), channel_id=1, source_target_pairs={{0,64},{32,96},{64,0},{96,32},{1,65},{33,97},{65,1},{97,33},{2,66}... | collective-permute-start | bytes 1474568 | tf_op jit(solution)/shard_map/ppermute | solution.py:835
  435.9 23.5 %collective-permute-start.57 = (bf16[384,640]{1,0:T(8,128)(2,1)S(1)}, bf16[384,640]{1,0:T(8,128)(2,1)}, u32[]{:S(2)}, u32[]{:S(2)}) collective-permute-start(bf16[384,640]{1,0:T(8,128)(2,1)S(1)} %get-tuple-element.320), channel_id=1, source_target_pairs={{0,32},{32,0},{64,96},{96,64},{1,33},{33,1},{65,97},{97,65},{2,34}... | collective-permute-start | bytes 1474568 | tf_op jit(solution)/shard_map/ppermute | solution.py:835
  463.2 14.6 %all-to-all-start.4 = ((bf16[4,96,640]{2,1,0:T(8,128)(2,1)}), bf16[4,96,640]{2,1,0:T(8,128)(2,1)S(1)}, u32[]{:S(2)}, u32[]{:S(2)}) async-start(bf16[4,96,640]{2,1,0:T(8,128)(2,1)} %bitcast.90), calls=%async_computation.6 | async-start | bytes 983040 | tf_op jit(solution)/shard_map/all_to_all | solution.py:833
  485.1 27.4 %all-to-all-start.5 = ((bf16[8,12,6400]{2,1,0:T(8,128)(2,1)}), bf16[8,12,6400]{2,1,0:T(8,128)(2,1)S(1)}, u32[]{:S(2)}, u32[]{:S(2)}) async-start(bf16[8,12,6400]{2,1,0:T(8,128)(2,1)} %reshape.490), calls=%async_computation.7 | async-start | bytes 3276800 | tf_op jit(solution)/shard_map/all_to_all | solution.py:578
  (97 other events, 879.2 us)
Sparse Core Ops, SparseCore 0:
  28.2 59.3 all-gather.4
  89.7 75.2 all-gather.6
  167.7 68.1 all-gather.8
  285.4 80.5 reduce-scatter.2
  369.7 104.0 reduce-scatter.4
